TPU v7x, 512 devices: a whole 4x4x16 slice. The times are simulated.
512 devices in a mesh: slab: 64 (over y, z), pencil: 8 (over x, core).
Axes of the slice: x: 4, y: 4, z: 16, core: 2. Of those that a mesh axis runs over, the one named last changes fastest.
Arguments:
- cell_x: int32 [2097152], P(('slab', 'pencil')), may hold values from 0 to 31
- cell_y: int32 [2097152], P(('slab', 'pencil')), may hold values from 0 to 7
- cell_z: int32 [2097152], P(('slab', 'pencil')), may hold values from 0 to 127
- offsets: float32 [3, 2097152], P(None, ('slab', 'pencil')), may hold values from 0 to 1
- radius_bin: int32 [2097152], P(('slab', 'pencil')), may hold values from 0 to 5
- masses: float32 [2097152], P(('slab', 'pencil')), may hold values from 4 to 64
- slab_dest: int32 [2097152], P(('slab', 'pencil')), may hold values from 0 to 63, as said below
- live_counts: int32 [512], P(('slab', 'pencil')), may hold values from 2048 to 4096, as said below
Outputs:
- spectrum: float32 [2, 2048, 64, 128], P(None, 'slab', 'pencil')
Inputs may be any that keep to these rules, and one draw needn't show every extreme that they name: `slab_dest`: among the 4096 rows of one device no slab is named more than 128 times, and one slab is named exactly 128 times by the rows of every device. Rows 0 to live_counts[b] - 1 of device b hold live particles; some device has all 4096 rows live.
All inputs are finite; a program needn't handle non-finite values.
Results may differ from a plain program's by a relative error of at most 0.003.
Values sent between devices are 32-bit elements; how exact they have to be, the bound alone decides.
No kernel may reach another device: no remote copies, remote signals or barrier semaphores. Data moves between devices by JAX's collectives and lax.ppermute only.
A program may use at most 64 MiB of HBM per device.

v0:
```python
import math

import jax
import jax.numpy as jnp
from jax import lax
from jax.sharding import PartitionSpec as P

NX = 2048
GHOST = 3
CY = 8
NZ = 128


def padded(value, sides, width):
    for axis, dim in sides:
        devices, length = (lax.axis_size(axis), value.shape[dim])
        up = [(i, (i + 1) % devices) for i in range(devices)]
        down = [(j, i) for i, j in up]
        last = lax.slice_in_dim(value, length - width, length, axis=dim)
        leading = lax.slice_in_dim(value, 0, width, axis=dim)
        before = lax.ppermute(last, axis, up)
        after = lax.ppermute(leading, axis, down)
        value = jnp.concatenate([before, value, after], axis=dim)
    return value


def swapped(block, axis, stride):
    count = lax.axis_size(axis)
    route = []
    for low in range(count):
        high = low | 1 << stride
        if high != low and high < count:
            route += [(low, high), (high, low)]
    return lax.ppermute(block, axis, route)


def kernel_weights(position, radius):
    base_cell = jnp.floor(position)
    fraction = position - base_cell
    tap_offsets = jnp.arange(-GHOST, GHOST + 1).astype(position.dtype)
    scaled_gap = (tap_offsets[None, :] + 0.5 - fraction[:, None]) / radius[:, None]
    bump_values = jnp.maximum(1.0 - scaled_gap * scaled_gap, 0.0)
    bump_values = bump_values * bump_values
    weights = bump_values / jnp.sum(bump_values, axis=1, keepdims=True)
    return (base_cell.astype(jnp.int32), weights)


def spread_taps(position, radius, width, shift_cells, periodic):
    base_cell, weights = kernel_weights(position, radius)
    columns = jnp.arange(width, dtype=jnp.int32)[None, :]
    spread = jnp.zeros((position.shape[0], width), jnp.float32)
    for tap_number in range(2 * GHOST + 1):
        target = base_cell + (tap_number - GHOST) + shift_cells
        if periodic:
            target = target % width
        spread = spread + jnp.where(
            target[:, None] == columns, weights[:, tap_number : tap_number + 1], 0.0
        )
    return spread


def plane_transform(real_part, imag_part, planes):
    grid_index = jnp.arange(planes, dtype=jnp.int32)
    product_table = grid_index[:, None] * grid_index[None, :] % planes
    angles = 2.0 * math.pi * product_table.astype(jnp.float32) / planes
    cosine_table = jnp.cos(angles)
    sine_table = jnp.sin(angles)
    highest = lax.Precision.HIGHEST
    out_real = jnp.einsum("ml,rlc->rmc", cosine_table, real_part, precision=highest) + jnp.einsum(
        "ml,rlc->rmc", sine_table, imag_part, precision=highest
    )
    out_imag = jnp.einsum("ml,rlc->rmc", cosine_table, imag_part, precision=highest) - jnp.einsum(
        "ml,rlc->rmc", sine_table, real_part, precision=highest
    )
    return (out_real, out_imag)


def local(cell_x, cell_y, cell_z, offsets, radius_bin, masses, slab_dest, live_counts):
    slab_count = lax.axis_size("slab")
    per_device = cell_x.shape[0]
    capacity = 2 * per_device // slab_count
    planes = NX // slab_count
    slot_index = jnp.arange(per_device, dtype=jnp.int32)
    weighted = jnp.where(slot_index < live_counts[0], masses, 0.0)
    fields = jnp.stack(
        [
            cell_x.astype(jnp.float32) + offsets[0],
            cell_y.astype(jnp.float32) + offsets[1],
            cell_z.astype(jnp.float32) + offsets[2],
            1.0 + 0.5 * radius_bin.astype(jnp.float32),
            weighted,
        ]
    )
    chosen = (slab_dest[:, None] == jnp.arange(slab_count, dtype=jnp.int32)[None, :]).astype(
        jnp.int32
    )
    slot_rank = jnp.sum((jnp.cumsum(chosen, axis=0) - chosen) * chosen, axis=1)
    slot_target = slab_dest * capacity + slot_rank
    outgoing = jnp.zeros((5, slab_count * capacity), jnp.float32).at[3].set(1.0)
    outgoing = outgoing.at[:, slot_target].set(fields).reshape(5, slab_count, capacity)
    arrived = lax.all_to_all(outgoing, "slab", split_axis=1, concat_axis=1, tiled=True).reshape(
        5, slab_count * capacity
    )
    slot_count = slab_count * capacity
    block_rows = min(512, slot_count)
    wide_first = planes + 2 * GHOST
    wide_second = CY + 2 * GHOST

    def deposit_block(block_index, deposit_grid):
        pieces = lax.dynamic_slice_in_dim(arrived, block_index * block_rows, block_rows, 1)
        along_first = spread_taps(pieces[0], pieces[3], wide_first, GHOST, False)
        along_second = spread_taps(pieces[1], pieces[3], wide_second, GHOST, False)
        along_third = spread_taps(pieces[2], pieces[3], NZ, 0, True)
        plane_weights = (
            along_first[:, :, None] * along_second[:, None, :] * pieces[4][:, None, None]
        ).astype(jnp.bfloat16)
        plane_weights = plane_weights.reshape(block_rows, wide_first * wide_second)
        depth_weights = along_third.astype(jnp.bfloat16)
        return deposit_grid + lax.dot_general(
            plane_weights,
            depth_weights,
            (((0,), (0,)), ((), ())),
            preferred_element_type=jnp.float32,
        )

    deposit_grid = lax.fori_loop(
        0,
        slot_count // block_rows,
        deposit_block,
        jnp.zeros((wide_first * wide_second, NZ), jnp.float32),
    )
    deposit_grid = deposit_grid.reshape(wide_first, wide_second, NZ)
    side_rims = jnp.concatenate([deposit_grid[:, :GHOST], deposit_grid[:, -GHOST:]], axis=1)
    side_arrived = padded(side_rims, (("pencil", 1),), GHOST)
    interior = deposit_grid[:, GHOST:-GHOST]
    interior = interior.at[:, :GHOST].add(side_arrived[:, :GHOST])
    interior = interior.at[:, -GHOST:].add(side_arrived[:, 3 * GHOST :])
    plane_rims = jnp.concatenate([interior[:GHOST], interior[-GHOST:]], axis=0)
    plane_arrived = padded(plane_rims, (("slab", 0),), GHOST)
    density = interior[GHOST:-GHOST]
    density = density.at[:GHOST].add(plane_arrived[:GHOST])
    density = density.at[-GHOST:].add(plane_arrived[3 * GHOST :])
    columns_real = density.reshape(planes, CY * NZ)
    scale = 1.0 / math.sqrt(NX)
    bit_count = slab_count.bit_length() - 1
    slab_index = lax.axis_index("slab")
    columns_imag = jnp.zeros_like(columns_real)
    for section_index in range(bit_count):
        bit_index = bit_count - 1 - section_index
        half_span = 1 << bit_index
        is_upper = jnp.right_shift(slab_index, bit_index) % 2 == 1
        phase = -2.0 * math.pi * (slab_index % half_span).astype(jnp.float32) / (2 * half_span)
        cosine = jnp.cos(phase)
        sine = jnp.sin(phase)
        if section_index == 0:
            partner_real = swapped(columns_real, "slab", bit_index)
            diff_real = partner_real - columns_real
            next_real = jnp.where(is_upper, diff_real * cosine, columns_real + partner_real)
            next_imag = jnp.where(is_upper, diff_real * sine, jnp.zeros_like(columns_real))
        else:
            partner_real, partner_imag = swapped((columns_real, columns_imag), "slab", bit_index)
            diff_real = partner_real - columns_real
            diff_imag = partner_imag - columns_imag
            next_real = jnp.where(
                is_upper, diff_real * cosine - diff_imag * sine, columns_real + partner_real
            )
            next_imag = jnp.where(
                is_upper, diff_real * sine + diff_imag * cosine, columns_imag + partner_imag
            )
        columns_real = next_real
        columns_imag = next_imag
    reversed_index = jnp.zeros((), jnp.int32)
    for bit_index in range(bit_count):
        reversed_index = reversed_index + jnp.right_shift(slab_index, bit_index) % 2 * (
            1 << bit_count - 1 - bit_index
        )
    plane_ids = jnp.arange(planes, dtype=jnp.int32)
    twiddle_steps = reversed_index * plane_ids % NX
    twiddle_angle = (-2.0 * math.pi * twiddle_steps.astype(jnp.float32) / NX)[:, None]
    rotated_real = columns_real * jnp.cos(twiddle_angle) - columns_imag * jnp.sin(twiddle_angle)
    rotated_imag = columns_real * jnp.sin(twiddle_angle) + columns_imag * jnp.cos(twiddle_angle)
    final_real, final_imag = plane_transform(rotated_real[None], rotated_imag[None], planes)
    out_real = final_real[0] * scale
    out_imag = final_imag[0] * scale
    return jnp.stack([out_real, out_imag]).reshape(2, planes, CY, NZ)


def solution(mesh):
    in_specs = (
        P(("slab", "pencil")),
        P(("slab", "pencil")),
        P(("slab", "pencil")),
        P(None, ("slab", "pencil")),
        P(("slab", "pencil")),
        P(("slab", "pencil")),
        P(("slab", "pencil")),
        P(("slab", "pencil")),
    )
    out_specs = P(None, "slab", "pencil", None)
    return jax.shard_map(local, mesh=mesh, in_specs=in_specs, out_specs=out_specs, check_vma=False)
```

profile of v0, /device:TPU:6, one launch (start us, length us, event | category | flops | bytes accessed | tf_op | source)
XLA Modules:
  0.0 242.9 jit_solution(17581858544929394707)
XLA Ops:
  7.5 18.4 %reduce-window.6 = s32[64,32,128]{2,1,0:T(8,128)S(1)} reduce-window(s32[64,32,128]{2,1,0:T(8,128)S(1)} %fusion.37, s32[]{:T(128)} %constant.513.clone.1), window={size=1x1x128 pad=0_0x0_0x127_0}, to_apply=%region_0.1 | reduce-window | flops 33292288 | bytes 2097156 | tf_op jit(solution)/shard_map/reduce-window
  28.2 4.4 %copy.43 = f32[5,8192]{0,1:T(8,128)} copy(f32[5,8192]{0,1:T(8,128)} %constant.520.clone.1) | data formatting | bytes 327680
  32.6 15.0 %scatter_fusion = f32[5,8192]{0,1:T(8,128)} fusion(f32[5,8192]{0,1:T(8,128)} %copy.43, s32[4096]{0:T(1024)S(1)} %compare_select_fusion, f32[4096,5]{1,0:T(8,128)} %copy.16), kind=kCustom, calls=%fused_computation | custom fusion | bytes 262144 | tf_op jit(solution)/shard_map/scatter | solution.py:100
  47.6 3.5 %copy.17 = f32[5,64,128]{2,0,1:T(8,128)} copy(f32[5,64,128]{0,2,1:T(8,128)} %bitcast.138) | data formatting | bytes 327680 | tf_op jit(solution)/shard_map/reshape | solution.py:100
  51.1 18.7 %all-to-all-start = ((f32[5,64,128]{2,0,1:T(8,128)}), f32[5,64,128]{2,0,1:T(8,128)S(1)}, u32[]{:S(2)}, u32[]{:S(2)}) async-start(f32[5,64,128]{2,0,1:T(8,128)} %copy.17), calls=%async_computation | async-start | bytes 524288 | tf_op jit(solution)/shard_map/all_to_all | solution.py:101
  69.9 21.0 %all-to-all-done = f32[5,64,128]{2,0,1:T(8,128)S(1)} async-done(((f32[5,64,128]{2,0,1:T(8,128)}), f32[5,64,128]{2,0,1:T(8,128)S(1)}, u32[]{:S(2)}, u32[]{:S(2)}) %all-to-all-start) | async-done | bytes 163872 | tf_op jit(solution)/shard_map/all_to_all | solution.py:101
  90.8 35.0 %while.22 = (s32[]{:T(128)}, f32[532,128]{1,0:T(8,128)S(1)}, f32[5,8192]{1,0:T(8,128)S(1)}, s32[]{:T(128)}, s32[]{:T(128)}, /*index=5*/s32[]{}, s32[]{:T(128)}, s32[]{:T(128)}, s32[]{}, s32[]{}, /*index=10*/s32[]{}) while((s32[]{:T(128)}, f32[532,128]{1,0:T(8,128)S(1)}, f32[5,8192]{1,0:T(8,128)S(1)}, s32[]{:T(128)}, s32[]{:T(128)}, ...), condition=%wide.region_8.9_spmd.clone, body=%wide.region_4.8_spmd.clone.sunk | while | flops 72797216 | bytes 5443901 | solution.py:126
  130.3 2.8 %collective-permute-start.2 = (f32[3,8,128]{2,1,0:T(8,128)S(1)}, f32[3,8,128]{2,1,0:T(8,128)S(1)}, u32[]{:S(2)}, u32[]{:S(2)}) collective-permute-start(f32[3,8,128]{2,1,0:T(8,128)S(1)} %get-tuple-element.291), channel_id=1, source_target_pairs={{0,8},{8,16},{16,24},{24,32},{32,40},{40,48},{48,56},{56,64},{64,7... | collective-permute-start | bytes 36872 | tf_op jit(solution)/shard_map/ppermute | solution.py:21
  133.2 6.4 %collective-permute-start.3 = (f32[3,8,128]{2,1,0:T(8,128)S(1)}, f32[3,8,128]{2,1,0:T(8,128)S(1)}, u32[]{:S(2)}, u32[]{:S(2)}) collective-permute-start(f32[3,8,128]{2,1,0:T(8,128)S(1)} %get-tuple-element.290), channel_id=1, source_target_pairs={{8,0},{16,8},{24,16},{32,24},{40,32},{48,40},{56,48},{64,56},{72,6... | collective-permute-start | bytes 36872 | tf_op jit(solution)/shard_map/ppermute | solution.py:22
  140.9 3.7 %collective-permute-start.4 = (f32[32,1024]{1,0:T(8,128)S(1)}, f32[32,1024]{1,0:T(8,128)S(1)}, u32[]{:S(2)}, u32[]{:S(2)}) collective-permute-start(f32[32,1024]{1,0:T(8,128)S(1)} %bitcast.171), channel_id=1, source_target_pairs={{0,256},{256,0},{8,264},{264,8},{16,272},{272,16},{24,280},{280,24... | collective-permute-start | bytes 393224 | tf_op jit(solution)/shard_map/ppermute | solution.py:34
  144.8 5.3 %collective-permute-done.4 = f32[32,1024]{1,0:T(8,128)S(1)} collective-permute-done((f32[32,1024]{1,0:T(8,128)S(1)}, f32[32,1024]{1,0:T(8,128)S(1)}, u32[]{:S(2)}, u32[]{:S(2)}) %collective-permute-start.4) | collective-permute-done | bytes 131104 | tf_op jit(solution)/shard_map/ppermute | solution.py:34
  152.3 3.7 %collective-permute-start.6 = (f32[32,1024]{1,0:T(8,128)S(1)}, f32[32,1024]{1,0:T(8,128)S(1)}, u32[]{:S(2)}, u32[]{:S(2)}) collective-permute-start(f32[32,1024]{1,0:T(8,128)S(1)} %get-tuple-element.289), channel_id=1, source_target_pairs={{0,128},{128,0},{8,136},{136,8},{16,144},{144,16},{24,152},{152,24... | collective-permute-start | bytes 393224 | tf_op jit(solution)/shard_map/ppermute | solution.py:34
  160.0 3.3 %collective-permute-start.7 = (f32[32,1024]{1,0:T(8,128)S(1)}, f32[32,1024]{1,0:T(8,128)S(1)}, u32[]{:S(2)}, u32[]{:S(2)}) collective-permute-start(f32[32,1024]{1,0:T(8,128)S(1)} %get-tuple-element.284), channel_id=1, source_target_pairs={{0,64},{64,0},{8,72},{72,8},{16,80},{80,16},{24,88},{88,24},{32,96... | collective-permute-start | bytes 393224 | tf_op jit(solution)/shard_map/ppermute | solution.py:34
  163.3 11.2 %collective-permute-start.8 = (f32[32,1024]{1,0:T(8,128)S(1)}, f32[32,1024]{1,0:T(8,128)S(1)}, u32[]{:S(2)}, u32[]{:S(2)}) collective-permute-start(f32[32,1024]{1,0:T(8,128)S(1)} %get-tuple-element.285), channel_id=1, source_target_pairs={{0,64},{64,0},{8,72},{72,8},{16,80},{80,16},{24,88},{88,24},{32,96... | collective-permute-start | bytes 393224 | tf_op jit(solution)/shard_map/ppermute | solution.py:34
  174.8 16.3 %collective-permute-done.7 = f32[32,1024]{1,0:T(8,128)S(1)} collective-permute-done((f32[32,1024]{1,0:T(8,128)S(1)}, f32[32,1024]{1,0:T(8,128)S(1)}, u32[]{:S(2)}, u32[]{:S(2)}) %collective-permute-start.7) | collective-permute-done | bytes 131104 | tf_op jit(solution)/shard_map/ppermute | solution.py:34
  191.1 2.5 %collective-permute-done.8 = f32[32,1024]{1,0:T(8,128)S(1)} collective-permute-done((f32[32,1024]{1,0:T(8,128)S(1)}, f32[32,1024]{1,0:T(8,128)S(1)}, u32[]{:S(2)}, u32[]{:S(2)}) %collective-permute-start.8) | collective-permute-done | bytes 131104 | tf_op jit(solution)/shard_map/ppermute | solution.py:34
  195.6 7.8 %collective-permute-start.9 = (f32[32,1024]{1,0:T(8,128)S(1)}, f32[32,1024]{1,0:T(8,128)S(1)}, u32[]{:S(2)}, u32[]{:S(2)}) collective-permute-start(f32[32,1024]{1,0:T(8,128)S(1)} %get-tuple-element.282), channel_id=1, source_target_pairs={{0,32},{32,0},{8,40},{40,8},{16,48},{48,16},{24,56},{56,24},{64,96... | collective-permute-start | bytes 393224 | tf_op jit(solution)/shard_map/ppermute | solution.py:34
  203.6 11.2 %collective-permute-done.10 = f32[32,1024]{1,0:T(8,128)S(1)} collective-permute-done((f32[32,1024]{1,0:T(8,128)S(1)}, f32[32,1024]{1,0:T(8,128)S(1)}, u32[]{:S(2)}, u32[]{:S(2)}) %collective-permute-start.10) | collective-permute-done | bytes 131104 | tf_op jit(solution)/shard_map/ppermute | solution.py:34
  214.9 2.7 %collective-permute-done.9 = f32[32,1024]{1,0:T(8,128)S(1)} collective-permute-done((f32[32,1024]{1,0:T(8,128)S(1)}, f32[32,1024]{1,0:T(8,128)S(1)}, u32[]{:S(2)}, u32[]{:S(2)}) %collective-permute-start.9) | collective-permute-done | bytes 131104 | tf_op jit(solution)/shard_map/ppermute | solution.py:34
  219.6 4.8 %collective-permute-start.12 = (f32[32,1024]{1,0:T(8,128)S(1)}, f32[32,1024]{1,0:T(8,128)S(1)}, u32[]{:S(2)}, u32[]{:S(2)}) collective-permute-start(f32[32,1024]{1,0:T(8,128)S(1)} %get-tuple-element.281), channel_id=1, source_target_pairs={{0,16},{16,0},{8,24},{24,8},{32,48},{48,32},{40,56},{56,40},{64,80... | collective-permute-start | bytes 393224 | tf_op jit(solution)/shard_map/ppermute | solution.py:34
  224.6 3.0 %collective-permute-done.11 = f32[32,1024]{1,0:T(8,128)S(1)} collective-permute-done((f32[32,1024]{1,0:T(8,128)S(1)}, f32[32,1024]{1,0:T(8,128)S(1)}, u32[]{:S(2)}, u32[]{:S(2)}) %collective-permute-start.11) | collective-permute-done | bytes 131104 | tf_op jit(solution)/shard_map/ppermute | solution.py:34
  227.6 2.7 %collective-permute-done.12 = f32[32,1024]{1,0:T(8,128)S(1)} collective-permute-done((f32[32,1024]{1,0:T(8,128)S(1)}, f32[32,1024]{1,0:T(8,128)S(1)}, u32[]{:S(2)}, u32[]{:S(2)}) %collective-permute-start.12) | collective-permute-done | bytes 131104 | tf_op jit(solution)/shard_map/ppermute | solution.py:34
  232.3 3.9 %collective-permute-start.14 = (f32[32,1024]{1,0:T(8,128)S(1)}, f32[32,1024]{1,0:T(8,128)S(1)}, u32[]{:S(2)}, u32[]{:S(2)}) collective-permute-start(f32[32,1024]{1,0:T(8,128)S(1)} %get-tuple-element.279), channel_id=1, source_target_pairs={{0,8},{8,0},{16,24},{24,16},{32,40},{40,32},{48,56},{56,48},{64,72... | collective-permute-start | bytes 393224 | tf_op jit(solution)/shard_map/ppermute | solution.py:34
  236.4 2.3 collective-permute-done.13
  (329 shorter events, 63.9 us)
Async XLA Ops:
  4.5 2.9 %copy-start = (s32[4096]{0:T(1024)S(1)}, s32[4096]{0:T(1024)}, u32[]{:S(2)}) copy-start(s32[4096]{0:T(1024)} %param.26) | copy-start | bytes 49156
  51.1 39.7 %all-to-all-start = ((f32[5,64,128]{2,0,1:T(8,128)}), f32[5,64,128]{2,0,1:T(8,128)S(1)}, u32[]{:S(2)}, u32[]{:S(2)}) async-start(f32[5,64,128]{2,0,1:T(8,128)} %copy.17), calls=%async_computation | async-start | bytes 524288 | tf_op jit(solution)/shard_map/all_to_all | solution.py:101
  125.9 3.8 %collective-permute-start = (f32[38,3,128]{2,1,0:T(4,128)S(1)}, f32[38,3,128]{2,1,0:T(4,128)S(1)}, u32[]{:S(2)}, u32[]{:S(2)}) collective-permute-start(f32[38,3,128]{2,1,0:T(4,128)S(1)} %get-tuple-element.287), channel_id=1, source_target_pairs={{0,1},{1,2},{2,3},{3,4},{4,5},{5,6},{6,7},{7,0},{8,9},{9,10},{10,1... | collective-permute-start | bytes 175112 | tf_op jit(solution)/shard_map/ppermute | solution.py:21
  126.0 4.1 %collective-permute-start.1 = (f32[38,3,128]{2,1,0:T(4,128)S(1)}, f32[38,3,128]{2,1,0:T(4,128)S(1)}, u32[]{:S(2)}, u32[]{:S(2)}) collective-permute-start(f32[38,3,128]{2,1,0:T(4,128)S(1)} %get-tuple-element.286), channel_id=1, source_target_pairs={{1,0},{2,1},{3,2},{4,3},{5,4},{6,5},{7,6},{0,7},{9,8},{10,9},{11,1... | collective-permute-start | bytes 175112 | tf_op jit(solution)/shard_map/ppermute | solution.py:22
  130.3 9.2 %collective-permute-start.2 = (f32[3,8,128]{2,1,0:T(8,128)S(1)}, f32[3,8,128]{2,1,0:T(8,128)S(1)}, u32[]{:S(2)}, u32[]{:S(2)}) collective-permute-start(f32[3,8,128]{2,1,0:T(8,128)S(1)} %get-tuple-element.291), channel_id=1, source_target_pairs={{0,8},{8,16},{16,24},{24,32},{32,40},{40,48},{48,56},{56,64},{64,7... | collective-permute-start | bytes 36872 | tf_op jit(solution)/shard_map/ppermute | solution.py:21
  133.2 7.7 %collective-permute-start.3 = (f32[3,8,128]{2,1,0:T(8,128)S(1)}, f32[3,8,128]{2,1,0:T(8,128)S(1)}, u32[]{:S(2)}, u32[]{:S(2)}) collective-permute-start(f32[3,8,128]{2,1,0:T(8,128)S(1)} %get-tuple-element.290), channel_id=1, source_target_pairs={{8,0},{16,8},{24,16},{32,24},{40,32},{48,40},{56,48},{64,56},{72,6... | collective-permute-start | bytes 36872 | tf_op jit(solution)/shard_map/ppermute | solution.py:22
  140.9 9.2 %collective-permute-start.4 = (f32[32,1024]{1,0:T(8,128)S(1)}, f32[32,1024]{1,0:T(8,128)S(1)}, u32[]{:S(2)}, u32[]{:S(2)}) collective-permute-start(f32[32,1024]{1,0:T(8,128)S(1)} %bitcast.171), channel_id=1, source_target_pairs={{0,256},{256,0},{8,264},{264,8},{16,272},{272,16},{24,280},{280,24... | collective-permute-start | bytes 393224 | tf_op jit(solution)/shard_map/ppermute | solution.py:34
  150.2 7.9 %collective-permute-start.5 = (f32[32,1024]{1,0:T(8,128)S(1)}, f32[32,1024]{1,0:T(8,128)S(1)}, u32[]{:S(2)}, u32[]{:S(2)}) collective-permute-start(f32[32,1024]{1,0:T(8,128)S(1)} %get-tuple-element.288), channel_id=1, source_target_pairs={{0,128},{128,0},{8,136},{136,8},{16,144},{144,16},{24,152},{152,24... | collective-permute-start | bytes 393224 | tf_op jit(solution)/shard_map/ppermute | solution.py:34
  152.3 7.6 %collective-permute-start.6 = (f32[32,1024]{1,0:T(8,128)S(1)}, f32[32,1024]{1,0:T(8,128)S(1)}, u32[]{:S(2)}, u32[]{:S(2)}) collective-permute-start(f32[32,1024]{1,0:T(8,128)S(1)} %get-tuple-element.289), channel_id=1, source_target_pairs={{0,128},{128,0},{8,136},{136,8},{16,144},{144,16},{24,152},{152,24... | collective-permute-start | bytes 393224 | tf_op jit(solution)/shard_map/ppermute | solution.py:34
  160.0 31.1 %collective-permute-start.7 = (f32[32,1024]{1,0:T(8,128)S(1)}, f32[32,1024]{1,0:T(8,128)S(1)}, u32[]{:S(2)}, u32[]{:S(2)}) collective-permute-start(f32[32,1024]{1,0:T(8,128)S(1)} %get-tuple-element.284), channel_id=1, source_target_pairs={{0,64},{64,0},{8,72},{72,8},{16,80},{80,16},{24,88},{88,24},{32,96... | collective-permute-start | bytes 393224 | tf_op jit(solution)/shard_map/ppermute | solution.py:34
  163.3 30.3 %collective-permute-start.8 = (f32[32,1024]{1,0:T(8,128)S(1)}, f32[32,1024]{1,0:T(8,128)S(1)}, u32[]{:S(2)}, u32[]{:S(2)}) collective-permute-start(f32[32,1024]{1,0:T(8,128)S(1)} %get-tuple-element.285), channel_id=1, source_target_pairs={{0,64},{64,0},{8,72},{72,8},{16,80},{80,16},{24,88},{88,24},{32,96... | collective-permute-start | bytes 393224 | tf_op jit(solution)/shard_map/ppermute | solution.py:34
  193.7 21.2 %collective-permute-start.10 = (f32[32,1024]{1,0:T(8,128)S(1)}, f32[32,1024]{1,0:T(8,128)S(1)}, u32[]{:S(2)}, u32[]{:S(2)}) collective-permute-start(f32[32,1024]{1,0:T(8,128)S(1)} %get-tuple-element.283), channel_id=1, source_target_pairs={{0,32},{32,0},{8,40},{40,8},{16,48},{48,16},{24,56},{56,24},{64,96... | collective-permute-start | bytes 393224 | tf_op jit(solution)/shard_map/ppermute | solution.py:34
  195.6 22.0 %collective-permute-start.9 = (f32[32,1024]{1,0:T(8,128)S(1)}, f32[32,1024]{1,0:T(8,128)S(1)}, u32[]{:S(2)}, u32[]{:S(2)}) collective-permute-start(f32[32,1024]{1,0:T(8,128)S(1)} %get-tuple-element.282), channel_id=1, source_target_pairs={{0,32},{32,0},{8,40},{40,8},{16,48},{48,16},{24,56},{56,24},{64,96... | collective-permute-start | bytes 393224 | tf_op jit(solution)/shard_map/ppermute | solution.py:34
  217.6 10.0 %collective-permute-start.11 = (f32[32,1024]{1,0:T(8,128)S(1)}, f32[32,1024]{1,0:T(8,128)S(1)}, u32[]{:S(2)}, u32[]{:S(2)}) collective-permute-start(f32[32,1024]{1,0:T(8,128)S(1)} %get-tuple-element.280), channel_id=1, source_target_pairs={{0,16},{16,0},{8,24},{24,8},{32,48},{48,32},{40,56},{56,40},{64,80... | collective-permute-start | bytes 393224 | tf_op jit(solution)/shard_map/ppermute | solution.py:34
  219.6 10.8 %collective-permute-start.12 = (f32[32,1024]{1,0:T(8,128)S(1)}, f32[32,1024]{1,0:T(8,128)S(1)}, u32[]{:S(2)}, u32[]{:S(2)}) collective-permute-start(f32[32,1024]{1,0:T(8,128)S(1)} %get-tuple-element.281), channel_id=1, source_target_pairs={{0,16},{16,0},{8,24},{24,8},{32,48},{48,32},{40,56},{56,40},{64,80... | collective-permute-start | bytes 393224 | tf_op jit(solution)/shard_map/ppermute | solution.py:34
  230.4 8.2 %collective-permute-start.13 = (f32[32,1024]{1,0:T(8,128)S(1)}, f32[32,1024]{1,0:T(8,128)S(1)}, u32[]{:S(2)}, u32[]{:S(2)}) collective-permute-start(f32[32,1024]{1,0:T(8,128)S(1)} %get-tuple-element.278), channel_id=1, source_target_pairs={{0,8},{8,0},{16,24},{24,16},{32,40},{40,32},{48,56},{56,48},{64,72... | collective-permute-start | bytes 393224 | tf_op jit(solution)/shard_map/ppermute | solution.py:34
  232.3 8.2 %collective-permute-start.14 = (f32[32,1024]{1,0:T(8,128)S(1)}, f32[32,1024]{1,0:T(8,128)S(1)}, u32[]{:S(2)}, u32[]{:S(2)}) collective-permute-start(f32[32,1024]{1,0:T(8,128)S(1)} %get-tuple-element.279), channel_id=1, source_target_pairs={{0,8},{8,0},{16,24},{24,16},{32,40},{40,32},{48,56},{56,48},{64,72... | collective-permute-start | bytes 393224 | tf_op jit(solution)/shard_map/ppermute | solution.py:34
where the time goes:
time: 244 us; the launch traced here: 243 us
  waiting for transfers between devices  76.2 us (31%)
  starting transfers between devices  76.1 us (31%)
  other arithmetic  32.5 us (13%)
  local copies, waits for them, and re-layouts  31.6 us (13%)
  matrix products  22.4 us (9%)
    ppermute x11, waiting for transfers between devices, swapped(): return lax.ppermute(block, axis, route)  51.8 us
    ppermute x11, starting transfers between devices, swapped(): return lax.ppermute(block, axis, route)  46.4 us
    all_to_all x1, waiting for transfers between devices, local(): lax.all_to_all(outgoing, 'slab', split_axis=1, concat_axis=1, tiled=True)  21 us
    dot_general x16, matrix products, deposit_block(): lax.dot_general(plane_weights, depth_weights, (((0,), (0,)), ((), ())), p...  20.9 us
    another operation x3, other arithmetic  19 us
    all_to_all x1, starting transfers between devices, local(): lax.all_to_all(outgoing, 'slab', split_axis=1, concat_axis=1, tiled=True)  18.7 us
    scatter x1, local copies, waits for them, and re-layouts, local(): outgoing.at[:, slot_target].set(fields).reshape(5, slab_count, capacity)  15 us
    ppermute x2, starting transfers between devices, padded(): after = lax.ppermute(leading, axis, down)  8.09 us
  transfers between devices with their start and end apart: 16, of which 14 were waited for; matrix products, arithmetic and copies ran while one was open for 0% of the time, Pallas kernels for 0%

commit v1 on v0

v1 whole, which is shorter than its diff:
```python
import math

import jax
import jax.numpy as jnp
import numpy as np
from jax import lax
from jax.experimental import pallas as pl
from jax.experimental.pallas import tpu as pltpu
from jax.sharding import PartitionSpec as P

NX = 2048
GHOST = 3
CY = 8
NZ = 128
SLABS = 64
PLANES = 32
LANES = 128
ROWS = 32
PIECES = 13
EXT = 40
GROUPS = EXT // 8
WIDE = CY + 2 * GHOST
VMEM = 48 * 1024 * 1024


def split3(value):
    high = value.astype(jnp.bfloat16).astype(jnp.float32)
    rest = value - high
    middle = rest.astype(jnp.bfloat16).astype(jnp.float32)
    return [high, middle, rest - middle]


def bucket_kernel(
    live, cell_x, cell_y, cell_z, offsets, radius_bin, masses, dest, out,
    pieces, chosen, counts, left, right,
):
    row = lax.broadcasted_iota(jnp.int32, (ROWS, LANES), 0)
    lane = lax.broadcasted_iota(jnp.int32, (ROWS, LANES), 1)
    weighted = jnp.where(row * LANES + lane < live[0], masses[...], 0.0)
    held = (
        split3(cell_x[...].astype(jnp.float32) + offsets[0])
        + split3(cell_y[...].astype(jnp.float32) + offsets[1])
        + split3(cell_z[...].astype(jnp.float32) + offsets[2])
        + split3(weighted)
        + [1.0 + 0.5 * radius_bin[...].astype(jnp.float32)]
    )
    for number, piece in enumerate(held):
        pieces[number] = piece
    slab = lax.broadcasted_iota(jnp.int32, (SLABS, LANES), 0)
    for k in range(ROWS):
        chosen[k * SLABS : (k + 1) * SLABS] = jnp.where(
            slab == dest[k : k + 1, :], 1.0, 0.0
        ).astype(jnp.bfloat16)
    first = lax.broadcasted_iota(jnp.int32, (LANES, 2 * LANES), 0)
    second = lax.broadcasted_iota(jnp.int32, (LANES, 2 * LANES), 1)
    before = jnp.where((first < second) | (second >= LANES), 1.0, 0.0).astype(jnp.bfloat16)
    counts[...] = jnp.dot(chosen[...], before, preferred_element_type=jnp.float32)
    base = jnp.zeros((SLABS, LANES), jnp.float32)
    pair = lax.broadcasted_iota(jnp.int32, (SLABS // 2, LANES), 0)
    low = lax.broadcasted_iota(jnp.int32, (2 * LANES, LANES), 0)
    for k in range(ROWS):
        target = dest[k : k + 1, :]
        found = counts[k * SLABS : (k + 1) * SLABS, :]
        rank = jnp.sum(
            jnp.where(slab == target, found[:, :LANES] + base, 0.0), axis=0, keepdims=True
        )
        base = base + found[:, LANES:]
        slot = jnp.bitwise_and(target, 1) * LANES + rank.astype(jnp.int32)
        span = slice(k * LANES, (k + 1) * LANES)
        right[:, span] = jnp.where(low == slot, 1.0, 0.0).astype(jnp.bfloat16)
        mask = pair == jnp.right_shift(target, 1)
        for number in range(PIECES):
            left[number * ROWS : (number + 1) * ROWS, span] = jnp.where(
                mask, pieces[number, k : k + 1, :], 0.0
            ).astype(jnp.bfloat16)
    sent = lax.dot_general(
        left[...], right[...], (((1,), (1,)), ((), ())), preferred_element_type=jnp.float32
    )
    for field in range(5):
        at = 3 * field * ROWS
        value = sent[at : at + ROWS]
        if field < 4:
            value = (value + sent[at + ROWS : at + 2 * ROWS]) + sent[at + 2 * ROWS : at + 3 * ROWS]
        out[:, 0, field, :] = value[:, :LANES]
        out[:, 1, field, :] = value[:, LANES:]


def tap_sum(position, inverse):
    fraction = position - jnp.floor(position)
    total = jnp.zeros_like(position)
    for tap in range(-GHOST, GHOST + 1):
        gap = (tap + 0.5 - fraction) * inverse
        bump = jnp.maximum(1.0 - gap * gap, 0.0)
        total = total + bump * bump
    return total


def bump_of(gap):
    value = jnp.maximum(1.0 - gap * gap, 0.0)
    return value * value


BLOCK = 2


def deposit_kernel(arrived, inner, lower, upper, held, total):
    inverse = 1.0 / jnp.maximum(arrived[:, 4, :], 1.0)
    held[0] = arrived[:, 0, :]
    held[1] = arrived[:, 1, :]
    held[2] = arrived[:, 2, :]
    held[3] = inverse
    held[4] = arrived[:, 3, :] / (tap_sum(held[0], inverse) * tap_sum(held[1], inverse))
    held[5] = 1.0 / tap_sum(held[2], inverse)
    total[...] = jnp.zeros_like(total)
    wide = BLOCK * LANES
    first = lax.broadcasted_iota(jnp.int32, (EXT, wide), 0).astype(jnp.float32) + (0.5 - GHOST)
    second = lax.broadcasted_iota(jnp.int32, (16, wide), 0).astype(jnp.float32) + (0.5 - GHOST)
    third = lax.broadcasted_iota(jnp.int32, (NZ, wide), 0).astype(jnp.float32) + 0.5

    def step(index, carry):
        def row(field):
            return jnp.concatenate(
                [held[field, pl.ds(index * BLOCK + part, 1), :] for part in range(BLOCK)], axis=1
            )

        scale = row(3)
        along_first = bump_of((first - row(0)) * scale) * row(4)
        along_second = bump_of((second - row(1)) * scale)
        away = jnp.abs(third - row(2))
        away = jnp.minimum(away, NZ - away)
        depth = (bump_of(away * scale) * row(5)).astype(jnp.bfloat16)
        plane = jnp.concatenate(
            [along_first * along_second[y : y + 1, :] for y in range(WIDE)], axis=0
        ).astype(jnp.bfloat16)
        total[...] += lax.dot_general(
            plane, depth, (((1,), (1,)), ((), ())), preferred_element_type=jnp.float32
        )
        return carry

    lax.fori_loop(0, SLABS // BLOCK, step, 0, unroll=2)
    lower[...] = total[: GHOST * EXT]
    inner[...] = total[GHOST * EXT : (GHOST + CY) * EXT]
    upper[...] = total[(GHOST + CY) * EXT :]


def join_kernel(inner, from_before, from_after, out):
    for y in range(CY):
        for group in range(GROUPS):
            value = inner[y * EXT + group * 8 : y * EXT + group * 8 + 8]
            if y < GHOST:
                at = y * EXT + group * 8
                value = value + from_before[at : at + 8]
            if y >= CY - GHOST:
                at = (y - CY + GHOST) * EXT + group * 8
                value = value + from_after[at : at + 8]
            out[y * 8 : y * 8 + 8, group, :] = value


def slab_kernel(table, value, out):
    for group in range(GROUPS - 1):
        rows = value[:, group, :]
        if group == 0:
            last = value[:, GROUPS - 1, :]
            rows = rows + jnp.concatenate([last[SLABS - 1 :], last[: SLABS - 1]], axis=0)
        result = jnp.dot(
            table[group], rows, precision=lax.Precision.HIGHEST, preferred_element_type=jnp.float32
        )
        out[:, group, :] = result[:SLABS]
        out[:, GROUPS - 1 + group, :] = result[SLABS:]


def plane_kernel(table, value, out):
    for y in range(CY):
        rows = value[y * 8 : y * 8 + 8].reshape(SLABS, LANES)
        out[:, y, :] = jnp.dot(
            table[...], rows, precision=lax.Precision.HIGHEST, preferred_element_type=jnp.float32
        )


def slab_tables():
    device = np.arange(SLABS)
    frequency = np.zeros(SLABS, np.int64)
    for bit in range(6):
        frequency += (device >> bit & 1) << 5 - bit
    offset = np.arange(8)[:, None] + 8 * np.arange(4)[None, :] - GHOST
    cell = PLANES * device[None, None, None, :] + offset[:, :, None, None]
    angle = 2.0 * np.pi * (frequency[None, None, :, None] * cell % NX) / NX
    table = np.concatenate([np.cos(angle), -np.sin(angle)], axis=2)
    return (table / math.sqrt(NX)).astype(np.float32)


def plane_table():
    offset = np.arange(8)[:, None] + 8 * np.arange(4)[None, :] - GHOST
    angle = 2.0 * np.pi * (np.arange(PLANES)[:, None, None] * offset[None] % PLANES) / PLANES
    real = np.stack([np.cos(angle), np.sin(angle)], axis=2)
    imag = np.stack([-np.sin(angle), np.cos(angle)], axis=2)
    return np.stack([real, imag]).reshape(2 * PLANES, 8 * 2 * 4).astype(np.float32)


def call(kernel, out, scratch=(), specs=None, flops=0, moved=0):
    return pl.pallas_call(
        kernel,
        out_shape=out,
        **({} if specs is None else {"in_specs": specs}),
        scratch_shapes=list(scratch),
        compiler_params=pltpu.CompilerParams(vmem_limit_bytes=VMEM),
        cost_estimate=pl.CostEstimate(flops=flops, bytes_accessed=moved, transcendentals=0),
    )


def shape(*dims):
    return jax.ShapeDtypeStruct(dims, jnp.float32)


def bucket(cell_x, cell_y, cell_z, offsets, radius_bin, masses, slab_dest, live_counts):
    whole = pl.BlockSpec(memory_space=pltpu.VMEM)
    block = (ROWS, LANES)
    return call(
        bucket_kernel,
        shape(SLABS // 2, 2, 5, LANES),
        [
            pltpu.VMEM((PIECES, ROWS, LANES), jnp.float32),
            pltpu.VMEM((ROWS * SLABS, LANES), jnp.bfloat16),
            pltpu.VMEM((ROWS * SLABS, 2 * LANES), jnp.float32),
            pltpu.VMEM((PIECES * ROWS, ROWS * LANES), jnp.bfloat16),
            pltpu.VMEM((2 * LANES, ROWS * LANES), jnp.bfloat16),
        ],
        [pl.BlockSpec(memory_space=pltpu.SMEM)] + [whole] * 7,
        flops=10**9,
        moved=10**6,
    )(
        live_counts,
        cell_x.reshape(block),
        cell_y.reshape(block),
        cell_z.reshape(block),
        offsets.reshape((3,) + block),
        radius_bin.reshape(block),
        masses.reshape(block),
        slab_dest.reshape(block),
    ).reshape(SLABS, 5, LANES)


def deposit(arrived):
    return call(
        deposit_kernel,
        (shape(CY * EXT, NZ), shape(GHOST * EXT, NZ), shape(GHOST * EXT, NZ)),
        [
            pltpu.VMEM((6, SLABS, LANES), jnp.float32),
            pltpu.VMEM((WIDE * EXT, NZ), jnp.float32),
        ],
        flops=10**9,
        moved=10**6,
    )(arrived)


def exchanged(value):
    return lax.all_to_all(value, "slab", split_axis=0, concat_axis=0, tiled=True)


def local(cell_x, cell_y, cell_z, offsets, radius_bin, masses, slab_dest, live_counts):
    outgoing = bucket(
        cell_x, cell_y, cell_z, offsets, radius_bin, masses, slab_dest, live_counts
    )
    arrived = exchanged(outgoing)
    inner, lower, upper = deposit(arrived)
    count = lax.axis_size("pencil")
    up = [(i, (i + 1) % count) for i in range(count)]
    down = [(j, i) for i, j in up]
    from_before = lax.ppermute(upper, "pencil", up)
    from_after = lax.ppermute(lower, "pencil", down)
    joined = call(join_kernel, shape(SLABS, GROUPS, LANES))(inner, from_before, from_after)
    crossing = exchanged(joined)
    offset = lax.axis_index("slab") % 8
    table = lax.dynamic_index_in_dim(jnp.asarray(slab_tables()), offset, 0, keepdims=False)
    partial = call(slab_kernel, shape(SLABS, 2 * (GROUPS - 1), LANES))(table, crossing)
    back = exchanged(partial)
    final = call(plane_kernel, shape(2 * PLANES, CY, NZ))(jnp.asarray(plane_table()), back)
    return final.reshape(2, PLANES, CY, NZ)


def solution(mesh):
    in_specs = (
        P(("slab", "pencil")),
        P(("slab", "pencil")),
        P(("slab", "pencil")),
        P(None, ("slab", "pencil")),
        P(("slab", "pencil")),
        P(("slab", "pencil")),
        P(("slab", "pencil")),
        P(("slab", "pencil")),
    )
    out_specs = P(None, "slab", "pencil", None)
    return jax.shard_map(local, mesh=mesh, in_specs=in_specs, out_specs=out_specs, check_vma=False)
```

time: 244 us -> 117 us (0.48)
  blocking collectives: 0 us -> 67.9 us
  starting transfers between devices: 76.1 us -> 8.2 us
  waiting for transfers between devices: 76.2 us -> 22 us
  other arithmetic: 32.5 us -> 0 us
  local copies, waits for them, and re-layouts: 31.6 us -> 6.13 us
  matrix products: 22.4 us -> 0 us
  Pallas kernels: 0 us -> 11.5 us
    all_to_all x0 -> x2, blocking collectives: none -> 67.9 us  [exchanged(): lax.all_to_all(value, 'slab', split_axis=0, concat_axis=0, tiled=True)]
    ppermute x15 -> x2, starting transfers between devices: 57.4 us -> 1.75 us  [the longest x1 1.73 us: local(): from_after = lax.ppermute(lower, 'pencil', down)]
    ppermute x15 -> x2, waiting for transfers between devices: 55.2 us -> 1.9 us  [the longest x1 1.9 us: local(): from_before = lax.ppermute(upper, 'pencil', up)]
    dot_general x20 -> x0, matrix products: 22.4 us -> none  [the longest x16 20.9 us: deposit_block(): lax.dot_general(plane_weights, depth_weights, (((0,), (0,)), ((), ())), p...]
    another operation x4 -> x0, other arithmetic: 19.7 us -> none
    scatter x1 -> x0, local copies, waits for them, and re-layouts: 15 us -> none  [local(): outgoing.at[:, slot_target].set(fields).reshape(5, slab_count, capacity)]
    all_to_all x1, starting transfers between devices: 18.7 us -> 6.45 us  [exchanged(): lax.all_to_all(value, 'slab', split_axis=0, concat_axis=0, tiled=True)]
    pallas_call x0 -> x5, Pallas kernels: none -> 11.5 us  [the longest x1 6.53 us: deposit(): call(deposit_kernel, (shape(CY * EXT, NZ), shape(GHOST * EXT, NZ), shape(...]
  transfers between devices with their start and end apart: 16 -> 3, of which waited for: 14 -> 2; matrix products, arithmetic and copies ran while one was open for 0% -> 1% of each run, Pallas kernels for 0% -> 0%
where the time goes in v1:
time: 117 us; the launch traced here: 116 us
  blocking collectives  67.9 us (58%)
  waiting for transfers between devices  22 us (19%)
  Pallas kernels  11.5 us (10%)
  starting transfers between devices  8.2 us (7%)
  local copies, waits for them, and re-layouts  6.13 us (5%)
    all_to_all x2, blocking collectives, exchanged(): lax.all_to_all(value, 'slab', split_axis=0, concat_axis=0, tiled=True)  67.9 us
    all_to_all x1, waiting for transfers between devices, exchanged(): lax.all_to_all(value, 'slab', split_axis=0, concat_axis=0, tiled=True)  20.1 us
    pallas_call x1, Pallas kernels, deposit(): call(deposit_kernel, (shape(CY * EXT, NZ), shape(GHOST * EXT, NZ), shape(...  6.53 us
    all_to_all x1, starting transfers between devices, exchanged(): lax.all_to_all(value, 'slab', split_axis=0, concat_axis=0, tiled=True)  6.45 us
    unnamed x15, local copies, waits for them, and re-layouts  5.15 us
    pallas_call x1, Pallas kernels, bucket(): call(bucket_kernel, shape(SLABS // 2, 2, 5, LANES), [pltpu.VMEM((PIECES,...  2.56 us
  transfers between devices with their start and end apart: 3, of which 2 were waited for; matrix products, arithmetic and copies ran while one was open for 1% of the time, Pallas kernels for 0%

profile of v1, /device:TPU:6, one launch (start us, length us, event | category | flops | bytes accessed | tf_op | source)
XLA Modules:
  0.0 116.4 jit_solution(5257086593340923548)
XLA Ops:
  0.7 0.8 copy.13
  1.5 0.0 copy-start.1
  1.5 0.7 copy-done.1
  2.2 0.7 copy-done.2
  2.9 0.7 copy-done.3
  3.7 0.7 copy-done.4
  4.4 0.7 copy-done.5
  5.1 0.7 copy-done.6
  5.8 2.6 %shard_map.100 = f32[32,2,5,128]{3,2,1,0:T(8,128)S(1)} custom-call(s32[1]{0:T(128)S(6)} %copy.14.live, s32[32,128]{1,0:T(8,128)S(1)} %bitcast.16, s32[32,128]{1,0:T(8,128)S(1)} %bitcast.17, s32[32,128]{1,0:T(8,128)S(1)} %bitcast.18, f32[3,32,128]{2,1,0:T(8,128)S(1)} %bitcast.15, s32[32,128]{1,0:T(8,128)S(1)} %bitcast.19, f32[32,128]{1,0:T(8,128)S(1)} %bitcast.20, ...), custom_call_target="tpu_custom_call" | custom-call | flops 1000000000 | bytes 1000000 | tf_op jit(solution)/shard_map/pallas_call | solution.py:218
  8.4 39.5 %all_to_all.15.arrived = f32[64,5,128]{2,1,0:T(8,128)S(1)} all-to-all(f32[64,5,128]{2,1,0:T(8,128)S(1)} %bitcast.14), channel_id=1, replica_groups=mesh['slab'=64,'pencil'=8] {'slab'}, dimensions={0} | all-to-all | bytes 327680 | tf_op jit(solution)/shard_map/all_to_all | solution.py:257
  47.9 6.5 %shard_map.101 = (f32[320,128]{1,0:T(8,128)S(1)}, f32[120,128]{1,0:T(8,128)S(1)}, f32[120,128]{1,0:T(8,128)S(1)}) custom-call(f32[64,5,128]{2,1,0:T(8,128)S(1)} %all_to_all.15.arrived), custom_call_target="tpu_custom_call" | custom-call | flops 1000000000 | bytes 1000000 | tf_op jit(solution)/shard_map/pallas_call | solution.py:244
  54.4 0.0 copy-start
  54.4 0.0 collective-permute-start
  54.5 1.7 %collective-permute-start.1 = (f32[120,128]{1,0:T(8,128)S(1)}, f32[120,128]{1,0:T(8,128)S(1)}, u32[]{:S(2)}, u32[]{:S(2)}) collective-permute-start(f32[120,128]{1,0:T(8,128)S(1)} %get-tuple-element.10), channel_id=1, source_target_pairs={{1,0},{2,1},{3,2},{4,3},{5,4},{6,5},{7,6},{0,7},{9,8},{10,9},{11,1... | collective-permute-start | bytes 184328 | tf_op jit(solution)/shard_map/ppermute | solution.py:270
  56.2 1.9 %collective-permute-done.from_before = f32[120,128]{1,0:T(8,128)S(1)} collective-permute-done((f32[120,128]{1,0:T(8,128)S(1)}, f32[120,128]{1,0:T(8,128)S(1)}, u32[]{:S(2)}, u32[]{:S(2)}) %collective-permute-start) | collective-permute-done | bytes 61472 | tf_op jit(solution)/shard_map/ppermute | solution.py:269
  58.1 0.0 collective-permute-done.1.from_after
  58.1 0.8 shard_map.102
  58.9 6.4 %all-to-all-start.1 = ((f32[64,5,128]{2,1,0:T(8,128)}), f32[64,5,128]{2,1,0:T(8,128)S(1)}, u32[]{:S(2)}, u32[]{:S(2)}) async-start(f32[64,5,128]{2,1,0:T(8,128)} %shard_map.102), calls=%async_computation.1 | async-start | bytes 524288 | tf_op jit(solution)/shard_map/all_to_all | solution.py:257
  65.4 1.0 dynamic-slice_bitcast_fusion.table
  66.4 20.1 %all-to-all-done.1.value = f32[64,5,128]{2,1,0:T(8,128)S(1)} async-done(((f32[64,5,128]{2,1,0:T(8,128)}), f32[64,5,128]{2,1,0:T(8,128)S(1)}, u32[]{:S(2)}, u32[]{:S(2)}) %all-to-all-start.1) | async-done | bytes 163872 | tf_op jit(solution)/shard_map/all_to_all | solution.py:257
  86.5 0.5 shard_map.103
  86.9 28.4 %all_to_all.16.value = f32[64,8,128]{2,1,0:T(8,128)S(1)} all-to-all(f32[64,8,128]{2,1,0:T(8,128)S(1)} %shard_map.103), channel_id=1, replica_groups=mesh['slab'=64,'pencil'=8] {'slab'}, dimensions={0} | all-to-all | bytes 524288 | tf_op jit(solution)/shard_map/all_to_all | solution.py:257
  115.3 0.0 copy-done
  115.3 1.1 shard_map.104
  (5 shorter events, 0.0 us)
Async XLA Ops:
  1.5 0.7 copy-start.1
  2.2 0.7 copy-start.2
  2.9 0.7 copy-start.3
  3.7 0.7 copy-start.4
  4.4 0.7 copy-start.5
  5.1 0.7 copy-start.6
  54.4 60.9 %copy-start = (f32[64,64]{1,0:T(8,128)S(1)}, f32[64,64]{1,0:T(8,128)}, u32[]{:S(2)}) copy-start(f32[64,64]{1,0:T(8,128)} %constant.28.clone.table) | copy-start | bytes 49156
  54.4 3.7 %collective-permute-start = (f32[120,128]{1,0:T(8,128)S(1)}, f32[120,128]{1,0:T(8,128)S(1)}, u32[]{:S(2)}, u32[]{:S(2)}) collective-permute-start(f32[120,128]{1,0:T(8,128)S(1)} %get-tuple-element.9), channel_id=1, source_target_pairs={{0,1},{1,2},{2,3},{3,4},{4,5},{5,6},{6,7},{7,0},{8,9},{9,10},{10,1... | collective-permute-start | bytes 184328 | tf_op jit(solution)/shard_map/ppermute | solution.py:269
  54.5 3.6 %collective-permute-start.1 = (f32[120,128]{1,0:T(8,128)S(1)}, f32[120,128]{1,0:T(8,128)S(1)}, u32[]{:S(2)}, u32[]{:S(2)}) collective-permute-start(f32[120,128]{1,0:T(8,128)S(1)} %get-tuple-element.10), channel_id=1, source_target_pairs={{1,0},{2,1},{3,2},{4,3},{5,4},{6,5},{7,6},{0,7},{9,8},{10,9},{11,1... | collective-permute-start | bytes 184328 | tf_op jit(solution)/shard_map/ppermute | solution.py:270
  58.9 27.5 %all-to-all-start.1 = ((f32[64,5,128]{2,1,0:T(8,128)}), f32[64,5,128]{2,1,0:T(8,128)S(1)}, u32[]{:S(2)}, u32[]{:S(2)}) async-start(f32[64,5,128]{2,1,0:T(8,128)} %shard_map.102), calls=%async_computation.1 | async-start | bytes 524288 | tf_op jit(solution)/shard_map/all_to_all | solution.py:257

commit v2 on v1

--- a/solution.py
+++ b/solution.py
@@ -30,22 +30,17 @@
     return [high, middle, rest - middle]
 
 
-def bucket_kernel(
-    live, cell_x, cell_y, cell_z, offsets, radius_bin, masses, dest, out,
-    pieces, chosen, counts, left, right,
-):
-    row = lax.broadcasted_iota(jnp.int32, (ROWS, LANES), 0)
-    lane = lax.broadcasted_iota(jnp.int32, (ROWS, LANES), 1)
-    weighted = jnp.where(row * LANES + lane < live[0], masses[...], 0.0)
-    held = (
-        split3(cell_x[...].astype(jnp.float32) + offsets[0])
-        + split3(cell_y[...].astype(jnp.float32) + offsets[1])
-        + split3(cell_z[...].astype(jnp.float32) + offsets[2])
-        + split3(weighted)
-        + [1.0 + 0.5 * radius_bin[...].astype(jnp.float32)]
-    )
-    for number, piece in enumerate(held):
-        pieces[number] = piece
+def bucket_kernel(live, *refs):
+    sources, out, staged = refs[:7], refs[7], refs[8:15]
+    shifts, pieces, chosen, counts, left, right, arrivals = refs[15:]
+    copies = [
+        pltpu.make_async_copy(source, place, arrivals.at[number])
+        for number, (source, place) in enumerate(zip(sources, staged, strict=True))
+    ]
+    for copy in copies:
+        copy.start()
+    dest, offsets, cell_x, cell_y, cell_z, radius_bin, masses = staged
+    copies[0].wait()
     slab = lax.broadcasted_iota(jnp.int32, (SLABS, LANES), 0)
     for k in range(ROWS):
         chosen[k * SLABS : (k + 1) * SLABS] = jnp.where(
@@ -55,6 +50,25 @@
     second = lax.broadcasted_iota(jnp.int32, (LANES, 2 * LANES), 1)
     before = jnp.where((first < second) | (second >= LANES), 1.0, 0.0).astype(jnp.bfloat16)
     counts[...] = jnp.dot(chosen[...], before, preferred_element_type=jnp.float32)
+    for copy in copies[1:]:
+        copy.wait()
+    for axis in range(3):
+        for k in range(ROWS):
+            shifts[axis, k : k + 1, :] = offsets[
+                axis : axis + 1, k * LANES : (k + 1) * LANES
+            ]
+    row = lax.broadcasted_iota(jnp.int32, (ROWS, LANES), 0)
+    lane = lax.broadcasted_iota(jnp.int32, (ROWS, LANES), 1)
+    weighted = jnp.where(row * LANES + lane < live[0], masses[...], 0.0)
+    held = (
+        split3(cell_x[...].astype(jnp.float32) + shifts[0])
+        + split3(cell_y[...].astype(jnp.float32) + shifts[1])
+        + split3(cell_z[...].astype(jnp.float32) + shifts[2])
+        + split3(weighted)
+        + [1.0 + 0.5 * radius_bin[...].astype(jnp.float32)]
+    )
+    for number, piece in enumerate(held):
+        pieces[number] = piece
     base = jnp.zeros((SLABS, LANES), jnp.float32)
     pair = lax.broadcasted_iota(jnp.int32, (SLABS // 2, LANES), 0)
     low = lax.broadcasted_iota(jnp.int32, (2 * LANES, LANES), 0)
@@ -65,10 +79,10 @@
             jnp.where(slab == target, found[:, :LANES] + base, 0.0), axis=0, keepdims=True
         )
         base = base + found[:, LANES:]
-        slot = jnp.bitwise_and(target, 1) * LANES + rank.astype(jnp.int32)
+        slot = jnp.right_shift(target, 5) * LANES + rank.astype(jnp.int32)
         span = slice(k * LANES, (k + 1) * LANES)
         right[:, span] = jnp.where(low == slot, 1.0, 0.0).astype(jnp.bfloat16)
-        mask = pair == jnp.right_shift(target, 1)
+        mask = pair == jnp.bitwise_and(target, SLABS // 2 - 1)
         for number in range(PIECES):
             left[number * ROWS : (number + 1) * ROWS, span] = jnp.where(
                 mask, pieces[number, k : k + 1, :], 0.0
@@ -81,8 +95,9 @@
         value = sent[at : at + ROWS]
         if field < 4:
             value = (value + sent[at + ROWS : at + 2 * ROWS]) + sent[at + 2 * ROWS : at + 3 * ROWS]
-        out[:, 0, field, :] = value[:, :LANES]
-        out[:, 1, field, :] = value[:, LANES:]
+        span = slice(field * LANES, (field + 1) * LANES)
+        out[: SLABS // 2, 0, span] = value[:, :LANES]
+        out[SLABS // 2 :, 0, span] = value[:, LANES:]
 
 
 def tap_sum(position, inverse):
@@ -103,13 +118,19 @@
 BLOCK = 2
 
 
-def deposit_kernel(arrived, inner, lower, upper, held, total):
-    inverse = 1.0 / jnp.maximum(arrived[:, 4, :], 1.0)
-    held[0] = arrived[:, 0, :]
-    held[1] = arrived[:, 1, :]
-    held[2] = arrived[:, 2, :]
+def deposit_kernel(place, arrived, tables, inner, near, far, table, held, total, arrival):
+    copy = pltpu.make_async_copy(tables.at[place[1]], table, arrival)
+    copy.start()
+
+    def field(number):
+        return arrived[:, 0, number * LANES : (number + 1) * LANES]
+
+    inverse = 1.0 / jnp.maximum(field(4), 1.0)
+    held[0] = field(0)
+    held[1] = field(1)
+    held[2] = field(2)
     held[3] = inverse
-    held[4] = arrived[:, 3, :] / (tap_sum(held[0], inverse) * tap_sum(held[1], inverse))
+    held[4] = field(3) / (tap_sum(held[0], inverse) * tap_sum(held[1], inverse))
     held[5] = 1.0 / tap_sum(held[2], inverse)
     total[...] = jnp.zeros_like(total)
     wide = BLOCK * LANES
@@ -138,29 +159,34 @@
         return carry
 
     lax.fori_loop(0, SLABS // BLOCK, step, 0, unroll=2)
-    lower[...] = total[: GHOST * EXT]
     inner[...] = total[GHOST * EXT : (GHOST + CY) * EXT]
-    upper[...] = total[(GHOST + CY) * EXT :]
-
-
-def join_kernel(inner, from_before, from_after, out):
+    even = place[0] == 0
+    lower = total[: GHOST * EXT]
+    upper = total[(GHOST + CY) * EXT :]
+    near[...] = jnp.where(even, upper, lower)
+    far[...] = jnp.where(even, lower, upper)
+    copy.wait()
+
+
+def join_kernel(place, inner, near, far, out):
+    even = place[0] == 0
     for y in range(CY):
         for group in range(GROUPS):
             value = inner[y * EXT + group * 8 : y * EXT + group * 8 + 8]
             if y < GHOST:
                 at = y * EXT + group * 8
-                value = value + from_before[at : at + 8]
+                value = value + jnp.where(even, far[at : at + 8], near[at : at + 8])
             if y >= CY - GHOST:
                 at = (y - CY + GHOST) * EXT + group * 8
-                value = value + from_after[at : at + 8]
-            out[y * 8 : y * 8 + 8, group, :] = value
+                value = value + jnp.where(even, near[at : at + 8], far[at : at + 8])
+            out[y * 8 : y * 8 + 8, 0, group * LANES : (group + 1) * LANES] = value
 
 
 def slab_kernel(table, value, out):
     for group in range(GROUPS - 1):
-        rows = value[:, group, :]
+        rows = value[:, 0, group * LANES : (group + 1) * LANES]
         if group == 0:
-            last = value[:, GROUPS - 1, :]
+            last = value[:, 0, (GROUPS - 1) * LANES :]
             rows = rows + jnp.concatenate([last[SLABS - 1 :], last[: SLABS - 1]], axis=0)
         result = jnp.dot(
             table[group], rows, precision=lax.Precision.HIGHEST, preferred_element_type=jnp.float32
@@ -213,44 +239,45 @@
 
 
 def bucket(cell_x, cell_y, cell_z, offsets, radius_bin, masses, slab_dest, live_counts):
-    whole = pl.BlockSpec(memory_space=pltpu.VMEM)
     block = (ROWS, LANES)
+    sources = [slab_dest.reshape(block), offsets] + [
+        value.reshape(block) for value in (cell_x, cell_y, cell_z, radius_bin, masses)
+    ]
     return call(
         bucket_kernel,
-        shape(SLABS // 2, 2, 5, LANES),
-        [
+        shape(SLABS, 1, 5 * LANES),
+        [pltpu.VMEM(value.shape, value.dtype) for value in sources]
+        + [
+            pltpu.VMEM((3, ROWS, LANES), jnp.float32),
             pltpu.VMEM((PIECES, ROWS, LANES), jnp.float32),
             pltpu.VMEM((ROWS * SLABS, LANES), jnp.bfloat16),
             pltpu.VMEM((ROWS * SLABS, 2 * LANES), jnp.float32),
             pltpu.VMEM((PIECES * ROWS, ROWS * LANES), jnp.bfloat16),
             pltpu.VMEM((2 * LANES, ROWS * LANES), jnp.bfloat16),
+            pltpu.SemaphoreType.DMA((7,)),
         ],
-        [pl.BlockSpec(memory_space=pltpu.SMEM)] + [whole] * 7,
+        [pl.BlockSpec(memory_space=pltpu.SMEM)] + [pl.BlockSpec(memory_space=pltpu.HBM)] * 7,
         flops=10**9,
         moved=10**6,
-    )(
-        live_counts,
-        cell_x.reshape(block),
-        cell_y.reshape(block),
-        cell_z.reshape(block),
-        offsets.reshape((3,) + block),
-        radius_bin.reshape(block),
-        masses.reshape(block),
-        slab_dest.reshape(block),
-    ).reshape(SLABS, 5, LANES)
-
-
-def deposit(arrived):
+    )(live_counts, *sources)
+
+
+def deposit(place, arrived):
+    here, smem = pl.BlockSpec(memory_space=pltpu.VMEM), pl.BlockSpec(memory_space=pltpu.SMEM)
+    tables = jnp.asarray(slab_tables())
+    rim = shape(GHOST * EXT, NZ)
     return call(
         deposit_kernel,
-        (shape(CY * EXT, NZ), shape(GHOST * EXT, NZ), shape(GHOST * EXT, NZ)),
+        (shape(CY * EXT, NZ), rim, rim, shape(*tables.shape[1:])),
         [
             pltpu.VMEM((6, SLABS, LANES), jnp.float32),
             pltpu.VMEM((WIDE * EXT, NZ), jnp.float32),
+            pltpu.SemaphoreType.DMA,
         ],
+        [smem, here, pl.BlockSpec(memory_space=pltpu.HBM)],
         flops=10**9,
         moved=10**6,
-    )(arrived)
+    )(place, arrived, tables)
 
 
 def exchanged(value):
@@ -262,16 +289,17 @@
         cell_x, cell_y, cell_z, offsets, radius_bin, masses, slab_dest, live_counts
     )
     arrived = exchanged(outgoing)
-    inner, lower, upper = deposit(arrived)
+    place = jnp.stack([lax.axis_index("pencil") % 2, lax.axis_index("slab") % 8])
+    inner, near, far, table = deposit(place, arrived)
     count = lax.axis_size("pencil")
-    up = [(i, (i + 1) % count) for i in range(count)]
-    down = [(j, i) for i, j in up]
-    from_before = lax.ppermute(upper, "pencil", up)
-    from_after = lax.ppermute(lower, "pencil", down)
-    joined = call(join_kernel, shape(SLABS, GROUPS, LANES))(inner, from_before, from_after)
+    across = [(i, (i + 1 if i % 2 else i - 1) % count) for i in range(count)]
+    from_far = lax.ppermute(far, "pencil", across)
+    from_near = lax.ppermute(near, "pencil", [(i, i ^ 1) for i in range(count)])
+    here, smem = pl.BlockSpec(memory_space=pltpu.VMEM), pl.BlockSpec(memory_space=pltpu.SMEM)
+    joined = call(
+        join_kernel, shape(SLABS, 1, GROUPS * LANES), specs=[smem] + [here] * 3
+    )(place, inner, from_near, from_far)
     crossing = exchanged(joined)
-    offset = lax.axis_index("slab") % 8
-    table = lax.dynamic_index_in_dim(jnp.asarray(slab_tables()), offset, 0, keepdims=False)
     partial = call(slab_kernel, shape(SLABS, 2 * (GROUPS - 1), LANES))(table, crossing)
     back = exchanged(partial)
     final = call(plane_kernel, shape(2 * PLANES, CY, NZ))(jnp.asarray(plane_table()), back)

time: 117 us -> 115 us (0.983)
  blocking collectives: 67.9 us -> 51.6 us
  starting transfers between devices: 8.2 us -> 23.5 us
  waiting for transfers between devices: 22 us -> 19.6 us
  Pallas kernels: 11.5 us -> 13.1 us
    all_to_all x2, blocking collectives: 67.9 us -> 51.6 us  [exchanged(): lax.all_to_all(value, 'slab', split_axis=0, concat_axis=0, tiled=True)]
    all_to_all x1, starting transfers between devices: 6.45 us -> 18.7 us  [exchanged(): lax.all_to_all(value, 'slab', split_axis=0, concat_axis=0, tiled=True)]
    all_to_all x1, waiting for transfers between devices: 20.1 us -> 16.9 us  [exchanged(): lax.all_to_all(value, 'slab', split_axis=0, concat_axis=0, tiled=True)]
    ppermute x2, starting transfers between devices: 1.75 us -> 4.76 us  [the longest x1 2.84 us: local(): from_far = lax.ppermute(far, 'pencil', across)]
    pallas_call x3, Pallas kernels: 9.9 us -> 11.6 us  [the longest x1 7.08 us: deposit(): call(deposit_kernel, (shape(CY * EXT, NZ), rim, rim, shape(*tables.shape[...]
    unnamed x15 -> x18, local copies, waits for them, and re-layouts: 5.15 us -> 5.14 us
  transfers between devices with their start and end apart: 3 -> 3, of which waited for: 2 -> 2; matrix products, arithmetic and copies ran while one was open for 1% -> 0% of each run, Pallas kernels for 0% -> 0%
where the time goes in v2:
time: 115 us; the launch traced here: 114 us
  blocking collectives  51.6 us (45%)
  starting transfers between devices  23.5 us (20%)
  waiting for transfers between devices  19.6 us (17%)
  Pallas kernels  13.1 us (11%)
  local copies, waits for them, and re-layouts  5.14 us (4%)
    all_to_all x2, blocking collectives, exchanged(): lax.all_to_all(value, 'slab', split_axis=0, concat_axis=0, tiled=True)  51.6 us
    all_to_all x1, starting transfers between devices, exchanged(): lax.all_to_all(value, 'slab', split_axis=0, concat_axis=0, tiled=True)  18.7 us
    all_to_all x1, waiting for transfers between devices, exchanged(): lax.all_to_all(value, 'slab', split_axis=0, concat_axis=0, tiled=True)  16.9 us
    pallas_call x1, Pallas kernels, deposit(): call(deposit_kernel, (shape(CY * EXT, NZ), rim, rim, shape(*tables.shape[...  7.08 us
    unnamed x18, local copies, waits for them, and re-layouts  5.14 us
    pallas_call x1, Pallas kernels, bucket(): call(bucket_kernel, shape(SLABS, 1, 5 * LANES), [pltpu.VMEM(value.shape,...  3.84 us
    ppermute x1, starting transfers between devices, local(): from_far = lax.ppermute(far, 'pencil', across)  2.84 us
    ppermute x1, waiting for transfers between devices, local(): from_far = lax.ppermute(far, 'pencil', across)  2.68 us
  transfers between devices with their start and end apart: 3, of which 2 were waited for; matrix products, arithmetic and copies ran while one was open for 0% of the time, Pallas kernels for 0%

profile of v2, /device:TPU:6, one launch (start us, length us, event | category | flops | bytes accessed | tf_op | source)
XLA Modules:
  0.0 113.7 jit_solution(446688073191357877)
XLA Ops:
  0.7 0.0 copy-start.1
  0.7 0.8 copy-done.1
  1.5 0.7 copy-done.2
  2.2 0.7 copy-done.3
  2.9 0.7 copy-done.4
  3.6 0.7 copy-done.5
  4.4 0.7 copy-done.6
  5.1 0.7 copy-done.7
  5.8 3.8 %shard_map.100 = f32[64,1,640]{2,1,0:T(1,128)} custom-call(s32[1]{0:T(128)S(6)} %copy.11.live, s32[32,128]{1,0:T(8,128)S(1)} %bitcast.9, f32[3,4096]{1,0:T(4,128)S(1)} %copy-done.1, s32[32,128]{1,0:T(8,128)S(1)} %bitcast.10, s32[32,128]{1,0:T(8,128)S(1)} %bitcast.11, s32[32,128]{1,0:T(8,128)S(1)} %bitcast.12, s32[32,128]{1,0:T(8,128)S(1)} %bitcast.13, ...), custom_call_target="tpu_custom_call" | custom-call | flops 1000000000 | bytes 1000000 | tf_op jit(solution)/shard_map/pallas_call | solution.py:246
  9.7 18.7 %all-to-all-start = ((f32[64,1,640]{2,1,0:T(1,128)}), f32[64,1,640]{2,1,0:T(1,128)S(1)}, u32[]{:S(2)}, u32[]{:S(2)}) async-start(f32[64,1,640]{2,1,0:T(1,128)} %shard_map.100), calls=%async_computation | async-start | bytes 327680 | tf_op jit(solution)/shard_map/all_to_all | solution.py:284
  28.4 0.1 pad_add_fusion.place
  28.5 16.9 %all-to-all-done.arrived = f32[64,1,640]{2,1,0:T(1,128)S(1)} async-done(((f32[64,1,640]{2,1,0:T(1,128)}), f32[64,1,640]{2,1,0:T(1,128)S(1)}, u32[]{:S(2)}, u32[]{:S(2)}) %all-to-all-start) | async-done | bytes 163872 | tf_op jit(solution)/shard_map/all_to_all | solution.py:284
  45.4 0.0 copy-done.8
  45.4 7.1 %shard_map.101 = (f32[320,128]{1,0:T(8,128)S(1)}, f32[120,128]{1,0:T(8,128)S(1)}, f32[120,128]{1,0:T(8,128)S(1)}, f32[4,128,64]{2,1,0:T(8,128)S(1)}) custom-call(s32[2]{0:T(128)S(1)} %pad_add_fusion.place, f32[64,1,640]{2,1,0:T(1,128)S(1)} %all-to-all-done.arrived, f32[8,4,128,64]{3,2,1,0:T(8,128)S(1)} %copy-done.8), custom_call_target="tpu_custom_call" | custom-call | flops 1000000000 | bytes 1000000 | tf_op jit(solution)/shard_map/pallas_call | solution.py:269
  52.5 1.9 %collective-permute-start = (f32[120,128]{1,0:T(8,128)S(1)}, f32[120,128]{1,0:T(8,128)S(1)}, u32[]{:S(2)}, u32[]{:S(2)}) collective-permute-start(f32[120,128]{1,0:T(8,128)S(1)} %get-tuple-element.11), channel_id=1, source_target_pairs={{0,1},{1,0},{2,3},{3,2},{4,5},{5,4},{6,7},{7,6},{8,9},{9,8},{10,11... | collective-permute-start | bytes 184328 | tf_op jit(solution)/shard_map/ppermute | solution.py:297
  54.4 2.8 %collective-permute-start.1 = (f32[120,128]{1,0:T(8,128)S(1)}, f32[120,128]{1,0:T(8,128)S(1)}, u32[]{:S(2)}, u32[]{:S(2)}) collective-permute-start(f32[120,128]{1,0:T(8,128)S(1)} %get-tuple-element.12), channel_id=1, source_target_pairs={{0,7},{1,2},{2,1},{3,4},{4,3},{5,6},{6,5},{7,0},{8,15},{9,10},{10,... | collective-permute-start | bytes 184328 | tf_op jit(solution)/shard_map/ppermute | solution.py:296
  57.2 0.0 collective-permute-done.near
  57.3 2.7 %collective-permute-done.1.far = f32[120,128]{1,0:T(8,128)S(1)} collective-permute-done((f32[120,128]{1,0:T(8,128)S(1)}, f32[120,128]{1,0:T(8,128)S(1)}, u32[]{:S(2)}, u32[]{:S(2)}) %collective-permute-start.1) | collective-permute-done | bytes 61472 | tf_op jit(solution)/shard_map/ppermute | solution.py:296
  59.9 0.6 shard_map.102
  60.6 23.7 %all_to_all.15.value = f32[64,1,640]{2,1,0:T(1,128)S(1)} all-to-all(f32[64,1,640]{2,1,0:T(1,128)S(1)} %shard_map.102), channel_id=1, replica_groups=mesh['slab'=64,'pencil'=8] {'slab'}, dimensions={0} | all-to-all | bytes 327680 | tf_op jit(solution)/shard_map/all_to_all | solution.py:284
  84.3 0.4 shard_map.103
  84.7 27.9 %all_to_all.16.value = f32[64,8,128]{2,1,0:T(8,128)S(1)} all-to-all(f32[64,8,128]{2,1,0:T(8,128)S(1)} %shard_map.103), channel_id=1, replica_groups=mesh['slab'=64,'pencil'=8] {'slab'}, dimensions={0} | all-to-all | bytes 524288 | tf_op jit(solution)/shard_map/all_to_all | solution.py:284
  112.6 0.0 copy-done
  112.6 1.1 shard_map.104
  (8 shorter events, 0.0 us)
Async XLA Ops:
  0.7 0.8 copy-start.1
  1.5 0.7 copy-start.2
  2.2 0.7 copy-start.3
  2.9 0.7 copy-start.4
  3.6 0.7 copy-start.5
  4.4 0.7 copy-start.6
  5.1 0.7 copy-start.7
  5.8 39.6 %copy-start.8 = (f32[8,4,128,64]{3,2,1,0:T(8,128)S(1)}, f32[8,4,128,64]{3,2,1,0:T(8,128)}, u32[]{:S(2)}) copy-start(f32[8,4,128,64]{3,2,1,0:T(8,128)} %constant.36.clone.tables) | copy-start | bytes 3145732
  9.7 35.7 %all-to-all-start = ((f32[64,1,640]{2,1,0:T(1,128)}), f32[64,1,640]{2,1,0:T(1,128)S(1)}, u32[]{:S(2)}, u32[]{:S(2)}) async-start(f32[64,1,640]{2,1,0:T(1,128)} %shard_map.100), calls=%async_computation | async-start | bytes 327680 | tf_op jit(solution)/shard_map/all_to_all | solution.py:284
  28.5 84.1 %copy-start = (f32[64,64]{1,0:T(8,128)S(1)}, f32[64,64]{1,0:T(8,128)}, u32[]{:S(2)}) copy-start(f32[64,64]{1,0:T(8,128)} %constant.37.clone.table) | copy-start | bytes 49156
  52.5 4.8 %collective-permute-start = (f32[120,128]{1,0:T(8,128)S(1)}, f32[120,128]{1,0:T(8,128)S(1)}, u32[]{:S(2)}, u32[]{:S(2)}) collective-permute-start(f32[120,128]{1,0:T(8,128)S(1)} %get-tuple-element.11), channel_id=1, source_target_pairs={{0,1},{1,0},{2,3},{3,2},{4,5},{5,4},{6,7},{7,6},{8,9},{9,8},{10,11... | collective-permute-start | bytes 184328 | tf_op jit(solution)/shard_map/ppermute | solution.py:297
  54.4 5.5 %collective-permute-start.1 = (f32[120,128]{1,0:T(8,128)S(1)}, f32[120,128]{1,0:T(8,128)S(1)}, u32[]{:S(2)}, u32[]{:S(2)}) collective-permute-start(f32[120,128]{1,0:T(8,128)S(1)} %get-tuple-element.12), channel_id=1, source_target_pairs={{0,7},{1,2},{2,1},{3,4},{4,3},{5,6},{6,5},{7,0},{8,15},{9,10},{10,... | collective-permute-start | bytes 184328 | tf_op jit(solution)/shard_map/ppermute | solution.py:296

commit v3 on v2

--- a/solution.py
+++ b/solution.py
@@ -20,7 +20,7 @@
 EXT = 40
 GROUPS = EXT // 8
 WIDE = CY + 2 * GHOST
-VMEM = 48 * 1024 * 1024
+VMEM = 40 * 1024 * 1024
 
 
 def split3(value):
@@ -118,8 +118,8 @@
 BLOCK = 2
 
 
-def deposit_kernel(place, arrived, tables, inner, near, far, table, held, total, arrival):
-    copy = pltpu.make_async_copy(tables.at[place[1]], table, arrival)
+def deposit_kernel(arrived, tables, inner, near, far, table, held, total, arrival):
+    copy = pltpu.make_async_copy(tables.at[lax.axis_index("slab") % 8], table, arrival)
     copy.start()
 
     def field(number):
@@ -160,7 +160,7 @@
 
     lax.fori_loop(0, SLABS // BLOCK, step, 0, unroll=2)
     inner[...] = total[GHOST * EXT : (GHOST + CY) * EXT]
-    even = place[0] == 0
+    even = lax.axis_index("pencil") % 2 == 0
     lower = total[: GHOST * EXT]
     upper = total[(GHOST + CY) * EXT :]
     near[...] = jnp.where(even, upper, lower)
@@ -168,8 +168,8 @@
     copy.wait()
 
 
-def join_kernel(place, inner, near, far, out):
-    even = place[0] == 0
+def join_kernel(inner, near, far, out):
+    even = lax.axis_index("pencil") % 2 == 0
     for y in range(CY):
         for group in range(GROUPS):
             value = inner[y * EXT + group * 8 : y * EXT + group * 8 + 8]
@@ -238,7 +238,7 @@
     return jax.ShapeDtypeStruct(dims, jnp.float32)
 
 
-def bucket(cell_x, cell_y, cell_z, offsets, radius_bin, masses, slab_dest, live_counts):
+def bucket(live_counts, cell_x, cell_y, cell_z, offsets, radius_bin, masses, slab_dest):
     block = (ROWS, LANES)
     sources = [slab_dest.reshape(block), offsets] + [
         value.reshape(block) for value in (cell_x, cell_y, cell_z, radius_bin, masses)
@@ -259,12 +259,12 @@
         [pl.BlockSpec(memory_space=pltpu.SMEM)] + [pl.BlockSpec(memory_space=pltpu.HBM)] * 7,
         flops=10**9,
         moved=10**6,
-    )(live_counts, *sources)
-
-
-def deposit(place, arrived):
-    here, smem = pl.BlockSpec(memory_space=pltpu.VMEM), pl.BlockSpec(memory_space=pltpu.SMEM)
-    tables = jnp.asarray(slab_tables())
+    )(live_counts, *[pltpu.with_memory_space_constraint(value, pltpu.HBM) for value in sources])
+
+
+def deposit(arrived):
+    here = pl.BlockSpec(memory_space=pltpu.VMEM)
+    tables = pltpu.with_memory_space_constraint(jnp.asarray(slab_tables()), pltpu.HBM)
     rim = shape(GHOST * EXT, NZ)
     return call(
         deposit_kernel,
@@ -274,10 +274,10 @@
             pltpu.VMEM((WIDE * EXT, NZ), jnp.float32),
             pltpu.SemaphoreType.DMA,
         ],
-        [smem, here, pl.BlockSpec(memory_space=pltpu.HBM)],
+        [here, pl.BlockSpec(memory_space=pltpu.HBM)],
         flops=10**9,
         moved=10**6,
-    )(place, arrived, tables)
+    )(arrived, tables)
 
 
 def exchanged(value):
@@ -286,19 +286,15 @@
 
 def local(cell_x, cell_y, cell_z, offsets, radius_bin, masses, slab_dest, live_counts):
     outgoing = bucket(
-        cell_x, cell_y, cell_z, offsets, radius_bin, masses, slab_dest, live_counts
+        live_counts, cell_x, cell_y, cell_z, offsets, radius_bin, masses, slab_dest
     )
     arrived = exchanged(outgoing)
-    place = jnp.stack([lax.axis_index("pencil") % 2, lax.axis_index("slab") % 8])
-    inner, near, far, table = deposit(place, arrived)
+    inner, near, far, table = deposit(arrived)
     count = lax.axis_size("pencil")
     across = [(i, (i + 1 if i % 2 else i - 1) % count) for i in range(count)]
     from_far = lax.ppermute(far, "pencil", across)
     from_near = lax.ppermute(near, "pencil", [(i, i ^ 1) for i in range(count)])
-    here, smem = pl.BlockSpec(memory_space=pltpu.VMEM), pl.BlockSpec(memory_space=pltpu.SMEM)
-    joined = call(
-        join_kernel, shape(SLABS, 1, GROUPS * LANES), specs=[smem] + [here] * 3
-    )(place, inner, from_near, from_far)
+    joined = call(join_kernel, shape(SLABS, 1, GROUPS * LANES))(inner, from_near, from_far)
     crossing = exchanged(joined)
     partial = call(slab_kernel, shape(SLABS, 2 * (GROUPS - 1), LANES))(table, crossing)
     back = exchanged(partial)

time: 115 us -> 107 us (0.930); the launches traced: 114 us -> 107 us
  blocking collectives: 51.6 us -> 87.1 us
  starting transfers between devices: 23.5 us -> 4.76 us
  waiting for transfers between devices: 19.6 us -> 2.69 us
  local copies, waits for them, and re-layouts: 5.14 us -> 0.01 us
  Pallas kernels: 13.1 us -> 11.9 us
    all_to_all x2 -> x3, blocking collectives: 51.6 us -> 87.1 us  [exchanged(): lax.all_to_all(value, 'slab', split_axis=0, concat_axis=0, tiled=True)]
    all_to_all x1 -> x0, starting transfers between devices: 18.7 us -> none  [exchanged(): lax.all_to_all(value, 'slab', split_axis=0, concat_axis=0, tiled=True)]
    all_to_all x1 -> x0, waiting for transfers between devices: 16.9 us -> none  [exchanged(): lax.all_to_all(value, 'slab', split_axis=0, concat_axis=0, tiled=True)]
    unnamed x18 -> x2, local copies, waits for them, and re-layouts: 5.14 us -> 0.01 us
  transfers between devices with their start and end apart: 3 -> 2, of which waited for: 2 -> 1; matrix products, arithmetic and copies ran while one was open for 0% -> 0% of each run, Pallas kernels for 0% -> 0%
where the time goes in v3:
time: 107 us
  blocking collectives  87.1 us (81%)
  Pallas kernels  11.9 us (11%)
  starting transfers between devices  4.76 us (4%)
  waiting for transfers between devices  2.69 us (3%)
    all_to_all x3, blocking collectives, exchanged(): lax.all_to_all(value, 'slab', split_axis=0, concat_axis=0, tiled=True)  87.1 us
    pallas_call x1, Pallas kernels, deposit(): call(deposit_kernel, (shape(CY * EXT, NZ), rim, rim, shape(*tables.shape[...  6.51 us
    pallas_call x1, Pallas kernels, bucket(): call(bucket_kernel, shape(SLABS, 1, 5 * LANES), [pltpu.VMEM(value.shape,...  3.71 us
    ppermute x1, starting transfers between devices, local(): from_far = lax.ppermute(far, 'pencil', across)  2.84 us
    ppermute x1, waiting for transfers between devices, local(): from_far = lax.ppermute(far, 'pencil', across)  2.68 us
  transfers between devices with their start and end apart: 2, of which 1 were waited for; matrix products, arithmetic and copies ran while one was open for 0% of the time, Pallas kernels for 0%

profile of v3, /device:TPU:6, one launch (start us, length us, event | category | flops | bytes accessed | tf_op | source)
XLA Modules:
  0.0 107.1 jit_solution(15009164006925703436)
XLA Ops:
  0.7 3.7 %shard_map.100 = f32[64,1,640]{2,1,0:T(1,128)S(1)} custom-call(s32[1]{0:T(128)S(6)} %copy.11.live, s32[32,128]{1,0:T(8,128)} %bitcast.7, f32[3,4096]{1,0:T(4,128)} %refs_1_.1, s32[32,128]{1,0:T(8,128)} %bitcast.8, s32[32,128]{1,0:T(8,128)} %bitcast.9, s32[32,128]{1,0:T(8,128)} %bitcast.10, s32[32,128]{1,0:T(8,128)} %bitcast.11, f32[32,128]{1,0:T(8,128)} %bitcast.12), custom_call_target="tpu_custom_call" | custom-call | flops 1000000000 | bytes 1000000 | tf_op jit(solution)/shard_map/pallas_call | solution.py:246
  4.4 35.5 %all_to_all.15.arrived = f32[64,1,640]{2,1,0:T(1,128)S(1)} all-to-all(f32[64,1,640]{2,1,0:T(1,128)S(1)} %shard_map.100), channel_id=1, replica_groups=mesh['slab'=64,'pencil'=8] {'slab'}, dimensions={0} | all-to-all | bytes 327680 | tf_op jit(solution)/shard_map/all_to_all | solution.py:284
  39.9 0.0 copy-start
  39.9 6.5 %shard_map.101 = (f32[320,128]{1,0:T(8,128)S(1)}, f32[120,128]{1,0:T(8,128)S(1)}, f32[120,128]{1,0:T(8,128)S(1)}, f32[4,128,64]{2,1,0:T(8,128)S(1)}) custom-call(f32[64,1,640]{2,1,0:T(1,128)S(1)} %all_to_all.15.arrived, f32[8,4,128,64]{3,2,1,0:T(8,128)} %constant.4.clone.tables), custom_call_target="tpu_custom_call" | custom-call | flops 1000000000 | bytes 1000000 | tf_op jit(solution)/shard_map/pallas_call | solution.py:269
  46.4 1.9 %collective-permute-start = (f32[120,128]{1,0:T(8,128)S(1)}, f32[120,128]{1,0:T(8,128)S(1)}, u32[]{:S(2)}, u32[]{:S(2)}) collective-permute-start(f32[120,128]{1,0:T(8,128)S(1)} %get-tuple-element.11), channel_id=1, source_target_pairs={{0,1},{1,0},{2,3},{3,2},{4,5},{5,4},{6,7},{7,6},{8,9},{9,8},{10,11... | collective-permute-start | bytes 184328 | tf_op jit(solution)/shard_map/ppermute | solution.py:296
  48.3 2.8 %collective-permute-start.1 = (f32[120,128]{1,0:T(8,128)S(1)}, f32[120,128]{1,0:T(8,128)S(1)}, u32[]{:S(2)}, u32[]{:S(2)}) collective-permute-start(f32[120,128]{1,0:T(8,128)S(1)} %get-tuple-element.12), channel_id=1, source_target_pairs={{0,7},{1,2},{2,1},{3,4},{4,3},{5,6},{6,5},{7,0},{8,15},{9,10},{10,... | collective-permute-start | bytes 184328 | tf_op jit(solution)/shard_map/ppermute | solution.py:295
  51.2 0.0 collective-permute-done.near
  51.2 2.7 %collective-permute-done.1.far = f32[120,128]{1,0:T(8,128)S(1)} collective-permute-done((f32[120,128]{1,0:T(8,128)S(1)}, f32[120,128]{1,0:T(8,128)S(1)}, u32[]{:S(2)}, u32[]{:S(2)}) %collective-permute-start.1) | collective-permute-done | bytes 61472 | tf_op jit(solution)/shard_map/ppermute | solution.py:295
  53.9 0.1 shard_map.102
  54.0 23.7 %all_to_all.16.value = f32[64,1,640]{2,1,0:T(1,128)S(1)} all-to-all(f32[64,1,640]{2,1,0:T(1,128)S(1)} %shard_map.102), channel_id=1, replica_groups=mesh['slab'=64,'pencil'=8] {'slab'}, dimensions={0} | all-to-all | bytes 327680 | tf_op jit(solution)/shard_map/all_to_all | solution.py:284
  77.7 0.4 shard_map.103
  78.1 27.9 %all_to_all.17.value = f32[64,8,128]{2,1,0:T(8,128)S(1)} all-to-all(f32[64,8,128]{2,1,0:T(8,128)S(1)} %shard_map.103), channel_id=1, replica_groups=mesh['slab'=64,'pencil'=8] {'slab'}, dimensions={0} | all-to-all | bytes 524288 | tf_op jit(solution)/shard_map/all_to_all | solution.py:284
  106.0 0.0 copy-done
  106.0 1.1 %shard_map.104 = f32[64,8,128]{2,1,0:T(8,128)} custom-call(f32[64,64]{1,0:T(8,128)S(1)} %copy-done, f32[64,8,128]{2,1,0:T(8,128)S(1)} %all_to_all.17.value), custom_call_target="tpu_custom_call" | custom-call | tf_op jit(solution)/shard_map/pallas_call | solution.py:301
Async XLA Ops:
  39.9 66.1 %copy-start = (f32[64,64]{1,0:T(8,128)S(1)}, f32[64,64]{1,0:T(8,128)}, u32[]{:S(2)}) copy-start(f32[64,64]{1,0:T(8,128)} %constant.5.clone.table) | copy-start | bytes 49156
  46.4 4.8 %collective-permute-start = (f32[120,128]{1,0:T(8,128)S(1)}, f32[120,128]{1,0:T(8,128)S(1)}, u32[]{:S(2)}, u32[]{:S(2)}) collective-permute-start(f32[120,128]{1,0:T(8,128)S(1)} %get-tuple-element.11), channel_id=1, source_target_pairs={{0,1},{1,0},{2,3},{3,2},{4,5},{5,4},{6,7},{7,6},{8,9},{9,8},{10,11... | collective-permute-start | bytes 184328 | tf_op jit(solution)/shard_map/ppermute | solution.py:296
  48.3 5.5 %collective-permute-start.1 = (f32[120,128]{1,0:T(8,128)S(1)}, f32[120,128]{1,0:T(8,128)S(1)}, u32[]{:S(2)}, u32[]{:S(2)}) collective-permute-start(f32[120,128]{1,0:T(8,128)S(1)} %get-tuple-element.12), channel_id=1, source_target_pairs={{0,7},{1,2},{2,1},{3,4},{4,3},{5,6},{6,5},{7,0},{8,15},{9,10},{10,... | collective-permute-start | bytes 184328 | tf_op jit(solution)/shard_map/ppermute | solution.py:295

commit v4 on v3

--- a/solution.py
+++ b/solution.py
@@ -115,10 +115,10 @@
     return value * value
 
 
-BLOCK = 2
-
-
-def deposit_kernel(arrived, tables, inner, near, far, table, held, total, arrival):
+BLOCK = 16
+
+
+def deposit_kernel(arrived, tables, inner, lower, upper, table, held, total, arrival):
     copy = pltpu.make_async_copy(tables.at[lax.axis_index("slab") % 8], table, arrival)
     copy.start()
 
@@ -160,25 +160,21 @@
 
     lax.fori_loop(0, SLABS // BLOCK, step, 0, unroll=2)
     inner[...] = total[GHOST * EXT : (GHOST + CY) * EXT]
-    even = lax.axis_index("pencil") % 2 == 0
-    lower = total[: GHOST * EXT]
-    upper = total[(GHOST + CY) * EXT :]
-    near[...] = jnp.where(even, upper, lower)
-    far[...] = jnp.where(even, lower, upper)
+    lower[...] = total[: GHOST * EXT]
+    upper[...] = total[(GHOST + CY) * EXT :]
     copy.wait()
 
 
-def join_kernel(inner, near, far, out):
-    even = lax.axis_index("pencil") % 2 == 0
+def join_kernel(inner, before, after, out):
     for y in range(CY):
         for group in range(GROUPS):
             value = inner[y * EXT + group * 8 : y * EXT + group * 8 + 8]
             if y < GHOST:
                 at = y * EXT + group * 8
-                value = value + jnp.where(even, far[at : at + 8], near[at : at + 8])
+                value = value + before[at : at + 8]
             if y >= CY - GHOST:
                 at = (y - CY + GHOST) * EXT + group * 8
-                value = value + jnp.where(even, near[at : at + 8], far[at : at + 8])
+                value = value + after[at : at + 8]
             out[y * 8 : y * 8 + 8, 0, group * LANES : (group + 1) * LANES] = value
 
 
@@ -195,12 +191,22 @@
         out[:, GROUPS - 1 + group, :] = result[SLABS:]
 
 
-def plane_kernel(table, value, out):
-    for y in range(CY):
-        rows = value[y * 8 : y * 8 + 8].reshape(SLABS, LANES)
-        out[:, y, :] = jnp.dot(
-            table[...], rows, precision=lax.Precision.HIGHEST, preferred_element_type=jnp.float32
+def plane_kernel(table, value, out, held, leaves):
+    rows = jnp.concatenate(
+        [value[y * 8 : y * 8 + 8].reshape(SLABS, LANES) for y in range(CY)], axis=1
+    )
+    copies = []
+    for part in range(2):
+        span = pl.ds(part * PLANES, PLANES)
+        result = jnp.dot(
+            table[span, :], rows, precision=lax.Precision.HIGHEST, preferred_element_type=jnp.float32
         )
+        for y in range(CY):
+            held[span, y, :] = result[:, y * LANES : (y + 1) * LANES]
+        copies.append(pltpu.make_async_copy(held.at[span], out.at[span], leaves.at[part]))
+        copies[part].start()
+    for copy in copies:
+        copy.wait()
 
 
 def slab_tables():
@@ -223,11 +229,12 @@
     return np.stack([real, imag]).reshape(2 * PLANES, 8 * 2 * 4).astype(np.float32)
 
 
-def call(kernel, out, scratch=(), specs=None, flops=0, moved=0):
+def call(kernel, out, scratch=(), specs=None, leave=None, flops=0, moved=0):
     return pl.pallas_call(
         kernel,
         out_shape=out,
         **({} if specs is None else {"in_specs": specs}),
+        **({} if leave is None else {"out_specs": leave}),
         scratch_shapes=list(scratch),
         compiler_params=pltpu.CompilerParams(vmem_limit_bytes=VMEM),
         cost_estimate=pl.CostEstimate(flops=flops, bytes_accessed=moved, transcendentals=0),
@@ -289,16 +296,21 @@
         live_counts, cell_x, cell_y, cell_z, offsets, radius_bin, masses, slab_dest
     )
     arrived = exchanged(outgoing)
-    inner, near, far, table = deposit(arrived)
+    inner, lower, upper, table = deposit(arrived)
     count = lax.axis_size("pencil")
-    across = [(i, (i + 1 if i % 2 else i - 1) % count) for i in range(count)]
-    from_far = lax.ppermute(far, "pencil", across)
-    from_near = lax.ppermute(near, "pencil", [(i, i ^ 1) for i in range(count)])
-    joined = call(join_kernel, shape(SLABS, 1, GROUPS * LANES))(inner, from_near, from_far)
+    up = [(i, (i + 1) % count) for i in range(count)]
+    before = lax.ppermute(upper, "pencil", up)
+    after = lax.ppermute(lower, "pencil", [(j, i) for i, j in up])
+    joined = call(join_kernel, shape(SLABS, 1, GROUPS * LANES))(inner, before, after)
     crossing = exchanged(joined)
     partial = call(slab_kernel, shape(SLABS, 2 * (GROUPS - 1), LANES))(table, crossing)
     back = exchanged(partial)
-    final = call(plane_kernel, shape(2 * PLANES, CY, NZ))(jnp.asarray(plane_table()), back)
+    final = call(
+        plane_kernel,
+        shape(2 * PLANES, CY, NZ),
+        [pltpu.VMEM((2 * PLANES, CY, NZ), jnp.float32), pltpu.SemaphoreType.DMA((2,))],
+        leave=pl.BlockSpec(memory_space=pltpu.HBM),
+    )(jnp.asarray(plane_table()), back)
     return final.reshape(2, PLANES, CY, NZ)
 
 

time: 107 us -> 101 us (0.944)
  starting transfers between devices: 4.76 us -> 1.75 us
  Pallas kernels: 11.9 us -> 9.15 us
    ppermute x2, starting transfers between devices: 4.76 us -> 1.75 us  [the longest x1 1.73 us: local(): after = lax.ppermute(lower, 'pencil', [(j, i) for i, j in up])]
    pallas_call x1, Pallas kernels: 6.51 us -> 3.82 us  [deposit(): call(deposit_kernel, (shape(CY * EXT, NZ), rim, rim, shape(*tables.shape[...]
where the time goes in v4:
time: 101 us
  blocking collectives  87.1 us (86%)
  Pallas kernels  9.15 us (9%)
  waiting for transfers between devices  1.9 us (2%)
  starting transfers between devices  1.75 us (2%)
    all_to_all x3, blocking collectives, exchanged(): lax.all_to_all(value, 'slab', split_axis=0, concat_axis=0, tiled=True)  87.1 us
    pallas_call x1, Pallas kernels, deposit(): call(deposit_kernel, (shape(CY * EXT, NZ), rim, rim, shape(*tables.shape[...  3.82 us
    pallas_call x1, Pallas kernels, bucket(): call(bucket_kernel, shape(SLABS, 1, 5 * LANES), [pltpu.VMEM(value.shape,...  3.71 us
  transfers between devices with their start and end apart: 2, of which 1 were waited for; matrix products, arithmetic and copies ran while one was open for 0% of the time, Pallas kernels for 0%

profile of v4, /device:TPU:6, one launch (start us, length us, event | category | flops | bytes accessed | tf_op | source)
XLA Modules:
  0.0 100.6 jit_solution(7874152367958662038)
XLA Ops:
  0.7 3.7 %shard_map.100 = f32[64,1,640]{2,1,0:T(1,128)S(1)} custom-call(s32[1]{0:T(128)S(6)} %copy.11.live, s32[32,128]{1,0:T(8,128)} %bitcast.7, f32[3,4096]{1,0:T(4,128)} %refs_1_.1, s32[32,128]{1,0:T(8,128)} %bitcast.8, s32[32,128]{1,0:T(8,128)} %bitcast.9, s32[32,128]{1,0:T(8,128)} %bitcast.10, s32[32,128]{1,0:T(8,128)} %bitcast.11, f32[32,128]{1,0:T(8,128)} %bitcast.12), custom_call_target="tpu_custom_call" | custom-call | flops 1000000000 | bytes 1000000 | tf_op jit(solution)/shard_map/pallas_call | solution.py:253
  4.4 35.5 %all_to_all.15.arrived = f32[64,1,640]{2,1,0:T(1,128)S(1)} all-to-all(f32[64,1,640]{2,1,0:T(1,128)S(1)} %shard_map.100), channel_id=1, replica_groups=mesh['slab'=64,'pencil'=8] {'slab'}, dimensions={0} | all-to-all | bytes 327680 | tf_op jit(solution)/shard_map/all_to_all | solution.py:291
  39.9 0.0 copy-start
  39.9 3.8 %shard_map.101 = (f32[320,128]{1,0:T(8,128)S(1)}, f32[120,128]{1,0:T(8,128)S(1)}, f32[120,128]{1,0:T(8,128)S(1)}, f32[4,128,64]{2,1,0:T(8,128)S(1)}) custom-call(f32[64,1,640]{2,1,0:T(1,128)S(1)} %all_to_all.15.arrived, f32[8,4,128,64]{3,2,1,0:T(8,128)} %constant.4.clone.tables), custom_call_target="tpu_custom_call" | custom-call | flops 1000000000 | bytes 1000000 | tf_op jit(solution)/shard_map/pallas_call | solution.py:276
  43.7 0.0 collective-permute-start
  43.7 1.7 %collective-permute-start.1 = (f32[120,128]{1,0:T(8,128)S(1)}, f32[120,128]{1,0:T(8,128)S(1)}, u32[]{:S(2)}, u32[]{:S(2)}) collective-permute-start(f32[120,128]{1,0:T(8,128)S(1)} %get-tuple-element.12), channel_id=1, source_target_pairs={{1,0},{2,1},{3,2},{4,3},{5,4},{6,5},{7,6},{0,7},{9,8},{10,9},{11,1... | collective-permute-start | bytes 184328 | tf_op jit(solution)/shard_map/ppermute | solution.py:303
  45.5 1.9 %collective-permute-done.before = f32[120,128]{1,0:T(8,128)S(1)} collective-permute-done((f32[120,128]{1,0:T(8,128)S(1)}, f32[120,128]{1,0:T(8,128)S(1)}, u32[]{:S(2)}, u32[]{:S(2)}) %collective-permute-start) | collective-permute-done | bytes 61472 | tf_op jit(solution)/shard_map/ppermute | solution.py:302
  47.4 0.0 collective-permute-done.1.after
  47.4 0.1 shard_map.102
  47.5 23.7 %all_to_all.16.value = f32[64,1,640]{2,1,0:T(1,128)S(1)} all-to-all(f32[64,1,640]{2,1,0:T(1,128)S(1)} %shard_map.102), channel_id=1, replica_groups=mesh['slab'=64,'pencil'=8] {'slab'}, dimensions={0} | all-to-all | bytes 327680 | tf_op jit(solution)/shard_map/all_to_all | solution.py:291
  71.1 0.4 shard_map.103
  71.6 27.9 %all_to_all.17.value = f32[64,8,128]{2,1,0:T(8,128)S(1)} all-to-all(f32[64,8,128]{2,1,0:T(8,128)S(1)} %shard_map.103), channel_id=1, replica_groups=mesh['slab'=64,'pencil'=8] {'slab'}, dimensions={0} | all-to-all | bytes 524288 | tf_op jit(solution)/shard_map/all_to_all | solution.py:291
  99.5 0.0 copy-done
  99.5 1.1 %shard_map.104 = f32[64,8,128]{2,1,0:T(8,128)} custom-call(f32[64,64]{1,0:T(8,128)S(1)} %copy-done, f32[64,8,128]{2,1,0:T(8,128)S(1)} %all_to_all.17.value), custom_call_target="tpu_custom_call" | custom-call | tf_op jit(solution)/shard_map/pallas_call | solution.py:308
Async XLA Ops:
  39.9 59.6 %copy-start = (f32[64,64]{1,0:T(8,128)S(1)}, f32[64,64]{1,0:T(8,128)}, u32[]{:S(2)}) copy-start(f32[64,64]{1,0:T(8,128)} %constant.5.clone.table) | copy-start | bytes 49156
  43.7 3.7 %collective-permute-start = (f32[120,128]{1,0:T(8,128)S(1)}, f32[120,128]{1,0:T(8,128)S(1)}, u32[]{:S(2)}, u32[]{:S(2)}) collective-permute-start(f32[120,128]{1,0:T(8,128)S(1)} %get-tuple-element.11), channel_id=1, source_target_pairs={{0,1},{1,2},{2,3},{3,4},{4,5},{5,6},{6,7},{7,0},{8,9},{9,10},{10,1... | collective-permute-start | bytes 184328 | tf_op jit(solution)/shard_map/ppermute | solution.py:302
  43.7 3.6 %collective-permute-start.1 = (f32[120,128]{1,0:T(8,128)S(1)}, f32[120,128]{1,0:T(8,128)S(1)}, u32[]{:S(2)}, u32[]{:S(2)}) collective-permute-start(f32[120,128]{1,0:T(8,128)S(1)} %get-tuple-element.12), channel_id=1, source_target_pairs={{1,0},{2,1},{3,2},{4,3},{5,4},{6,5},{7,6},{0,7},{9,8},{10,9},{11,1... | collective-permute-start | bytes 184328 | tf_op jit(solution)/shard_map/ppermute | solution.py:303

commit v5 on v4

--- a/solution.py
+++ b/solution.py
@@ -118,10 +118,7 @@
 BLOCK = 16
 
 
-def deposit_kernel(arrived, tables, inner, lower, upper, table, held, total, arrival):
-    copy = pltpu.make_async_copy(tables.at[lax.axis_index("slab") % 8], table, arrival)
-    copy.start()
-
+def deposit_rows(arrived, held, total, wanted):
     def field(number):
         return arrived[:, 0, number * LANES : (number + 1) * LANES]
 
@@ -151,7 +148,7 @@
         away = jnp.minimum(away, NZ - away)
         depth = (bump_of(away * scale) * row(5)).astype(jnp.bfloat16)
         plane = jnp.concatenate(
-            [along_first * along_second[y : y + 1, :] for y in range(WIDE)], axis=0
+            [along_first * along_second[y : y + 1, :] for y in wanted], axis=0
         ).astype(jnp.bfloat16)
         total[...] += lax.dot_general(
             plane, depth, (((1,), (1,)), ((), ())), preferred_element_type=jnp.float32
@@ -159,9 +156,18 @@
         return carry
 
     lax.fori_loop(0, SLABS // BLOCK, step, 0, unroll=2)
-    inner[...] = total[GHOST * EXT : (GHOST + CY) * EXT]
+
+
+def rim_kernel(arrived, lower, upper, held, total):
+    deposit_rows(arrived, held, total, [*range(GHOST), *range(GHOST + CY, WIDE)])
     lower[...] = total[: GHOST * EXT]
-    upper[...] = total[(GHOST + CY) * EXT :]
+    upper[...] = total[GHOST * EXT :]
+
+
+def inner_kernel(arrived, tables, inner, table, held, arrival):
+    copy = pltpu.make_async_copy(tables.at[lax.axis_index("slab") % 8], table, arrival)
+    copy.start()
+    deposit_rows(arrived, held, inner, range(GHOST, GHOST + CY))
     copy.wait()
 
 
@@ -269,19 +275,22 @@
     )(live_counts, *[pltpu.with_memory_space_constraint(value, pltpu.HBM) for value in sources])
 
 
-def deposit(arrived):
-    here = pl.BlockSpec(memory_space=pltpu.VMEM)
+HELD = pltpu.VMEM((6, SLABS, LANES), jnp.float32)
+
+
+def deposit_rims(arrived):
+    rim = shape(GHOST * EXT, NZ)
+    scratch = [HELD, pltpu.VMEM((2 * GHOST * EXT, NZ), jnp.float32)]
+    return call(rim_kernel, (rim, rim), scratch, flops=5 * 10**8, moved=10**6)(arrived)
+
+
+def deposit_inner(arrived):
     tables = pltpu.with_memory_space_constraint(jnp.asarray(slab_tables()), pltpu.HBM)
-    rim = shape(GHOST * EXT, NZ)
     return call(
-        deposit_kernel,
-        (shape(CY * EXT, NZ), rim, rim, shape(*tables.shape[1:])),
-        [
-            pltpu.VMEM((6, SLABS, LANES), jnp.float32),
-            pltpu.VMEM((WIDE * EXT, NZ), jnp.float32),
-            pltpu.SemaphoreType.DMA,
-        ],
-        [here, pl.BlockSpec(memory_space=pltpu.HBM)],
+        inner_kernel,
+        (shape(CY * EXT, NZ), shape(*tables.shape[1:])),
+        [HELD, pltpu.SemaphoreType.DMA],
+        [pl.BlockSpec(memory_space=pltpu.VMEM), pl.BlockSpec(memory_space=pltpu.HBM)],
         flops=10**9,
         moved=10**6,
     )(arrived, tables)
@@ -296,11 +305,12 @@
         live_counts, cell_x, cell_y, cell_z, offsets, radius_bin, masses, slab_dest
     )
     arrived = exchanged(outgoing)
-    inner, lower, upper, table = deposit(arrived)
+    lower, upper = deposit_rims(arrived)
     count = lax.axis_size("pencil")
     up = [(i, (i + 1) % count) for i in range(count)]
     before = lax.ppermute(upper, "pencil", up)
     after = lax.ppermute(lower, "pencil", [(j, i) for i, j in up])
+    inner, table = deposit_inner(arrived)
     joined = call(join_kernel, shape(SLABS, 1, GROUPS * LANES))(inner, before, after)
     crossing = exchanged(joined)
     partial = call(slab_kernel, shape(SLABS, 2 * (GROUPS - 1), LANES))(table, crossing)

time: 101 us -> 100 us (0.990)
  Pallas kernels: 9.15 us -> 11.9 us
  waiting for transfers between devices: 1.9 us -> 0.01 us
  blocking collectives: 87.1 us -> 85.7 us
    pallas_call x1 -> x2, Pallas kernels: 3.82 us -> 6.54 us  [the longest x1 3.46 us: deposit_inner(): call(inner_kernel, (shape(CY * EXT, NZ), shape(*tables.shape[1:])), [HELD...]
    ppermute x1, waiting for transfers between devices: 1.9 us -> 0.01 us  [local(): before = lax.ppermute(upper, 'pencil', up)]
    all_to_all x3, blocking collectives: 87.1 us -> 85.7 us  [exchanged(): lax.all_to_all(value, 'slab', split_axis=0, concat_axis=0, tiled=True)]
  transfers between devices with their start and end apart: 2 -> 2, of which waited for: 1 -> 0; matrix products, arithmetic and copies ran while one was open for 0% -> 0% of each run, Pallas kernels for 0% -> 3%
where the time goes in v5:
time: 100 us
  blocking collectives  85.7 us (86%)
  Pallas kernels  11.9 us (12%)
  starting transfers between devices  1.74 us (2%)
    all_to_all x3, blocking collectives, exchanged(): lax.all_to_all(value, 'slab', split_axis=0, concat_axis=0, tiled=True)  85.7 us
    pallas_call x1, Pallas kernels, bucket(): call(bucket_kernel, shape(SLABS, 1, 5 * LANES), [pltpu.VMEM(value.shape,...  3.71 us
    pallas_call x1, Pallas kernels, deposit_inner(): call(inner_kernel, (shape(CY * EXT, NZ), shape(*tables.shape[1:])), [HELD...  3.46 us
    pallas_call x1, Pallas kernels, deposit_rims(): call(rim_kernel, (rim, rim), scratch, flops=5 * 10 ** 8, moved=10 ** 6)  3.09 us
  transfers between devices with their start and end apart: 2, of which 0 were waited for; matrix products, arithmetic and copies ran while one was open for 0% of the time, Pallas kernels for 3%

profile of v5, /device:TPU:6, one launch (start us, length us, event | category | flops | bytes accessed | tf_op | source)
XLA Modules:
  0.0 100.1 jit_solution(10905635982272397384)
XLA Ops:
  0.7 3.7 %shard_map.100 = f32[64,1,640]{2,1,0:T(1,128)S(1)} custom-call(s32[1]{0:T(128)S(6)} %copy.11.live, s32[32,128]{1,0:T(8,128)} %bitcast.7, f32[3,4096]{1,0:T(4,128)} %refs_1_.1, s32[32,128]{1,0:T(8,128)} %bitcast.8, s32[32,128]{1,0:T(8,128)} %bitcast.9, s32[32,128]{1,0:T(8,128)} %bitcast.10, s32[32,128]{1,0:T(8,128)} %bitcast.11, f32[32,128]{1,0:T(8,128)} %bitcast.12), custom_call_target="tpu_custom_call" | custom-call | flops 1000000000 | bytes 1000000 | tf_op jit(solution)/shard_map/pallas_call | solution.py:259
  4.4 35.5 %all_to_all.15.arrived = f32[64,1,640]{2,1,0:T(1,128)S(1)} all-to-all(f32[64,1,640]{2,1,0:T(1,128)S(1)} %shard_map.100), channel_id=1, replica_groups=mesh['slab'=64,'pencil'=8] {'slab'}, dimensions={0} | all-to-all | bytes 327680 | tf_op jit(solution)/shard_map/all_to_all | solution.py:300
  39.9 3.1 %shard_map.102 = (f32[120,128]{1,0:T(8,128)S(1)}, f32[120,128]{1,0:T(8,128)S(1)}) custom-call(f32[64,1,640]{2,1,0:T(1,128)S(1)} %all_to_all.15.arrived), custom_call_target="tpu_custom_call" | custom-call | flops 500000000 | bytes 1000000 | tf_op jit(solution)/shard_map/pallas_call | solution.py:284
  43.0 0.0 collective-permute-start
  43.0 0.0 copy-start
  43.0 1.7 %collective-permute-start.1 = (f32[120,128]{1,0:T(8,128)S(1)}, f32[120,128]{1,0:T(8,128)S(1)}, u32[]{:S(2)}, u32[]{:S(2)}) collective-permute-start(f32[120,128]{1,0:T(8,128)S(1)} %get-tuple-element.12), channel_id=1, source_target_pairs={{1,0},{2,1},{3,2},{4,3},{5,4},{6,5},{7,6},{0,7},{9,8},{10,9},{11,1... | collective-permute-start | bytes 184328 | tf_op jit(solution)/shard_map/ppermute | solution.py:312
  44.7 3.5 %shard_map.101 = (f32[320,128]{1,0:T(8,128)S(1)}, f32[4,128,64]{2,1,0:T(8,128)S(1)}) custom-call(f32[64,1,640]{2,1,0:T(1,128)S(1)} %all_to_all.15.arrived, f32[8,4,128,64]{3,2,1,0:T(8,128)} %constant.4.clone.tables), custom_call_target="tpu_custom_call" | custom-call | flops 1000000000 | bytes 1000000 | tf_op jit(solution)/shard_map/pallas_call | solution.py:289
  48.2 0.0 collective-permute-done.before
  48.2 0.0 collective-permute-done.1.after
  48.2 0.1 shard_map.103
  48.3 23.4 %all_to_all.16.value = f32[64,1,640]{2,1,0:T(1,128)S(1)} all-to-all(f32[64,1,640]{2,1,0:T(1,128)S(1)} %shard_map.103), channel_id=1, replica_groups=mesh['slab'=64,'pencil'=8] {'slab'}, dimensions={0} | all-to-all | bytes 327680 | tf_op jit(solution)/shard_map/all_to_all | solution.py:300
  71.7 0.4 shard_map.104
  72.2 26.8 %all_to_all.17.value = f32[64,8,128]{2,1,0:T(8,128)S(1)} all-to-all(f32[64,8,128]{2,1,0:T(8,128)S(1)} %shard_map.104), channel_id=1, replica_groups=mesh['slab'=64,'pencil'=8] {'slab'}, dimensions={0} | all-to-all | bytes 524288 | tf_op jit(solution)/shard_map/all_to_all | solution.py:300
  99.0 0.0 copy-done
  99.0 1.1 %shard_map.105 = f32[64,8,128]{2,1,0:T(8,128)} custom-call(f32[64,64]{1,0:T(8,128)S(1)} %copy-done, f32[64,8,128]{2,1,0:T(8,128)S(1)} %all_to_all.17.value), custom_call_target="tpu_custom_call" | custom-call | tf_op jit(solution)/shard_map/pallas_call | solution.py:318
Async XLA Ops:
  43.0 5.2 %collective-permute-start = (f32[120,128]{1,0:T(8,128)S(1)}, f32[120,128]{1,0:T(8,128)S(1)}, u32[]{:S(2)}, u32[]{:S(2)}) collective-permute-start(f32[120,128]{1,0:T(8,128)S(1)} %get-tuple-element.11), channel_id=1, source_target_pairs={{0,1},{1,2},{2,3},{3,4},{4,5},{5,6},{6,7},{7,0},{8,9},{9,10},{10,1... | collective-permute-start | bytes 184328 | tf_op jit(solution)/shard_map/ppermute | solution.py:311
  43.0 56.0 %copy-start = (f32[64,64]{1,0:T(8,128)S(1)}, f32[64,64]{1,0:T(8,128)}, u32[]{:S(2)}) copy-start(f32[64,64]{1,0:T(8,128)} %constant.5.clone.table) | copy-start | bytes 49156
  43.0 5.2 %collective-permute-start.1 = (f32[120,128]{1,0:T(8,128)S(1)}, f32[120,128]{1,0:T(8,128)S(1)}, u32[]{:S(2)}, u32[]{:S(2)}) collective-permute-start(f32[120,128]{1,0:T(8,128)S(1)} %get-tuple-element.12), channel_id=1, source_target_pairs={{1,0},{2,1},{3,2},{4,3},{5,4},{6,5},{7,6},{0,7},{9,8},{10,9},{11,1... | collective-permute-start | bytes 184328 | tf_op jit(solution)/shard_map/ppermute | solution.py:312

commit v6 on v5

--- a/solution.py
+++ b/solution.py
@@ -16,18 +16,16 @@
 PLANES = 32
 LANES = 128
 ROWS = 32
-PIECES = 13
+PIECES = 11
 EXT = 40
 GROUPS = EXT // 8
 WIDE = CY + 2 * GHOST
 VMEM = 40 * 1024 * 1024
 
 
-def split3(value):
+def split2(value):
     high = value.astype(jnp.bfloat16).astype(jnp.float32)
-    rest = value - high
-    middle = rest.astype(jnp.bfloat16).astype(jnp.float32)
-    return [high, middle, rest - middle]
+    return [high, value - high]
 
 
 def bucket_kernel(live, *refs):
@@ -60,13 +58,15 @@
     row = lax.broadcasted_iota(jnp.int32, (ROWS, LANES), 0)
     lane = lax.broadcasted_iota(jnp.int32, (ROWS, LANES), 1)
     weighted = jnp.where(row * LANES + lane < live[0], masses[...], 0.0)
-    held = (
-        split3(cell_x[...].astype(jnp.float32) + shifts[0])
-        + split3(cell_y[...].astype(jnp.float32) + shifts[1])
-        + split3(cell_z[...].astype(jnp.float32) + shifts[2])
-        + split3(weighted)
-        + [1.0 + 0.5 * radius_bin[...].astype(jnp.float32)]
-    )
+    held = [
+        (cell_x[...] + PLANES * radius_bin[...]).astype(jnp.float32),
+        cell_y[...].astype(jnp.float32),
+        cell_z[...].astype(jnp.float32),
+        *split2(shifts[0]),
+        *split2(shifts[1]),
+        *split2(shifts[2]),
+        *split2(weighted),
+    ]
     for number, piece in enumerate(held):
         pieces[number] = piece
     base = jnp.zeros((SLABS, LANES), jnp.float32)
@@ -90,11 +90,16 @@
     sent = lax.dot_general(
         left[...], right[...], (((1,), (1,)), ((), ())), preferred_element_type=jnp.float32
     )
-    for field in range(5):
-        at = 3 * field * ROWS
-        value = sent[at : at + ROWS]
-        if field < 4:
-            value = (value + sent[at + ROWS : at + 2 * ROWS]) + sent[at + 2 * ROWS : at + 3 * ROWS]
+    part = [sent[number * ROWS : (number + 1) * ROWS] for number in range(PIECES)]
+    bins = jnp.floor(part[0] * (1.0 / PLANES))
+    values = [
+        (part[0] - PLANES * bins) + (part[3] + part[4]),
+        part[1] + (part[5] + part[6]),
+        part[2] + (part[7] + part[8]),
+        part[9] + part[10],
+        1.0 + 0.5 * bins,
+    ]
+    for field, value in enumerate(values):
         span = slice(field * LANES, (field + 1) * LANES)
         out[: SLABS // 2, 0, span] = value[:, :LANES]
         out[SLABS // 2 :, 0, span] = value[:, LANES:]
@@ -113,6 +118,11 @@
 def bump_of(gap):
     value = jnp.maximum(1.0 - gap * gap, 0.0)
     return value * value
+
+
+def around(gap):
+    gap = jnp.abs(gap)
+    return jnp.minimum(gap, NZ - gap)
 
 
 BLOCK = 16
@@ -144,8 +154,8 @@
         scale = row(3)
         along_first = bump_of((first - row(0)) * scale) * row(4)
         along_second = bump_of((second - row(1)) * scale)
-        away = jnp.abs(third - row(2))
-        away = jnp.minimum(away, NZ - away)
+        away = third - row(2)
+        away = jnp.concatenate([around(away[:8]), away[8 : NZ - 8], around(away[NZ - 8 :])], axis=0)
         depth = (bump_of(away * scale) * row(5)).astype(jnp.bfloat16)
         plane = jnp.concatenate(
             [along_first * along_second[y : y + 1, :] for y in wanted], axis=0

time: 100 us -> 99.9 us (level)
  no operation moved by 1% of the time
where the time goes in v6:
time: 99.9 us; the launch traced here: 99.6 us
  blocking collectives  86 us (86%)
  Pallas kernels  11.1 us (11%)
  starting transfers between devices  1.74 us (2%)
    all_to_all x3, blocking collectives, exchanged(): lax.all_to_all(value, 'slab', split_axis=0, concat_axis=0, tiled=True)  86 us
    pallas_call x1, Pallas kernels, bucket(): call(bucket_kernel, shape(SLABS, 1, 5 * LANES), [pltpu.VMEM(value.shape,...  3.57 us
    pallas_call x1, Pallas kernels, deposit_inner(): call(inner_kernel, (shape(CY * EXT, NZ), shape(*tables.shape[1:])), [HELD...  3.12 us
    pallas_call x1, Pallas kernels, deposit_rims(): call(rim_kernel, (rim, rim), scratch, flops=5 * 10 ** 8, moved=10 ** 6)  2.83 us
  transfers between devices with their start and end apart: 2, of which 0 were waited for; matrix products, arithmetic and copies ran while one was open for 0% of the time, Pallas kernels for 3%

profile of v6, /device:TPU:6, one launch (start us, length us, event | category | flops | bytes accessed | tf_op | source)
XLA Modules:
  0.0 99.6 jit_solution(7520505209469729651)
XLA Ops:
  0.7 3.6 %shard_map.100 = f32[64,1,640]{2,1,0:T(1,128)S(1)} custom-call(s32[1]{0:T(128)S(6)} %copy.11.live, s32[32,128]{1,0:T(8,128)} %bitcast.7, f32[3,4096]{1,0:T(4,128)} %refs_1_.1, s32[32,128]{1,0:T(8,128)} %bitcast.8, s32[32,128]{1,0:T(8,128)} %bitcast.9, s32[32,128]{1,0:T(8,128)} %bitcast.10, s32[32,128]{1,0:T(8,128)} %bitcast.11, f32[32,128]{1,0:T(8,128)} %bitcast.12), custom_call_target="tpu_custom_call" | custom-call | flops 1000000000 | bytes 1000000 | tf_op jit(solution)/shard_map/pallas_call | solution.py:269
  4.2 35.5 %all_to_all.15.arrived = f32[64,1,640]{2,1,0:T(1,128)S(1)} all-to-all(f32[64,1,640]{2,1,0:T(1,128)S(1)} %shard_map.100), channel_id=1, replica_groups=mesh['slab'=64,'pencil'=8] {'slab'}, dimensions={0} | all-to-all | bytes 327680 | tf_op jit(solution)/shard_map/all_to_all | solution.py:310
  39.7 2.8 %shard_map.102 = (f32[120,128]{1,0:T(8,128)S(1)}, f32[120,128]{1,0:T(8,128)S(1)}) custom-call(f32[64,1,640]{2,1,0:T(1,128)S(1)} %all_to_all.15.arrived), custom_call_target="tpu_custom_call" | custom-call | flops 500000000 | bytes 1000000 | tf_op jit(solution)/shard_map/pallas_call | solution.py:294
  42.6 0.0 collective-permute-start
  42.6 0.0 copy-start
  42.6 1.7 %collective-permute-start.1 = (f32[120,128]{1,0:T(8,128)S(1)}, f32[120,128]{1,0:T(8,128)S(1)}, u32[]{:S(2)}, u32[]{:S(2)}) collective-permute-start(f32[120,128]{1,0:T(8,128)S(1)} %get-tuple-element.12), channel_id=1, source_target_pairs={{1,0},{2,1},{3,2},{4,3},{5,4},{6,5},{7,6},{0,7},{9,8},{10,9},{11,1... | collective-permute-start | bytes 184328 | tf_op jit(solution)/shard_map/ppermute | solution.py:322
  44.3 3.1 %shard_map.101 = (f32[320,128]{1,0:T(8,128)S(1)}, f32[4,128,64]{2,1,0:T(8,128)S(1)}) custom-call(f32[64,1,640]{2,1,0:T(1,128)S(1)} %all_to_all.15.arrived, f32[8,4,128,64]{3,2,1,0:T(8,128)} %constant.4.clone.tables), custom_call_target="tpu_custom_call" | custom-call | flops 1000000000 | bytes 1000000 | tf_op jit(solution)/shard_map/pallas_call | solution.py:299
  47.5 0.0 collective-permute-done.before
  47.5 0.0 collective-permute-done.1.after
  47.5 0.1 shard_map.103
  47.6 23.8 %all_to_all.16.value = f32[64,1,640]{2,1,0:T(1,128)S(1)} all-to-all(f32[64,1,640]{2,1,0:T(1,128)S(1)} %shard_map.103), channel_id=1, replica_groups=mesh['slab'=64,'pencil'=8] {'slab'}, dimensions={0} | all-to-all | bytes 327680 | tf_op jit(solution)/shard_map/all_to_all | solution.py:310
  71.4 0.4 shard_map.104
  71.8 26.7 %all_to_all.17.value = f32[64,8,128]{2,1,0:T(8,128)S(1)} all-to-all(f32[64,8,128]{2,1,0:T(8,128)S(1)} %shard_map.104), channel_id=1, replica_groups=mesh['slab'=64,'pencil'=8] {'slab'}, dimensions={0} | all-to-all | bytes 524288 | tf_op jit(solution)/shard_map/all_to_all | solution.py:310
  98.5 0.0 copy-done
  98.5 1.1 %shard_map.105 = f32[64,8,128]{2,1,0:T(8,128)} custom-call(f32[64,64]{1,0:T(8,128)S(1)} %copy-done, f32[64,8,128]{2,1,0:T(8,128)S(1)} %all_to_all.17.value), custom_call_target="tpu_custom_call" | custom-call | tf_op jit(solution)/shard_map/pallas_call | solution.py:328
Async XLA Ops:
  42.6 4.9 %collective-permute-start = (f32[120,128]{1,0:T(8,128)S(1)}, f32[120,128]{1,0:T(8,128)S(1)}, u32[]{:S(2)}, u32[]{:S(2)}) collective-permute-start(f32[120,128]{1,0:T(8,128)S(1)} %get-tuple-element.11), channel_id=1, source_target_pairs={{0,1},{1,2},{2,3},{3,4},{4,5},{5,6},{6,7},{7,0},{8,9},{9,10},{10,1... | collective-permute-start | bytes 184328 | tf_op jit(solution)/shard_map/ppermute | solution.py:321
  42.6 55.9 %copy-start = (f32[64,64]{1,0:T(8,128)S(1)}, f32[64,64]{1,0:T(8,128)}, u32[]{:S(2)}) copy-start(f32[64,64]{1,0:T(8,128)} %constant.5.clone.table) | copy-start | bytes 49156
  42.6 4.9 %collective-permute-start.1 = (f32[120,128]{1,0:T(8,128)S(1)}, f32[120,128]{1,0:T(8,128)S(1)}, u32[]{:S(2)}, u32[]{:S(2)}) collective-permute-start(f32[120,128]{1,0:T(8,128)S(1)} %get-tuple-element.12), channel_id=1, source_target_pairs={{1,0},{2,1},{3,2},{4,3},{5,4},{6,5},{7,6},{0,7},{9,8},{10,9},{11,1... | collective-permute-start | bytes 184328 | tf_op jit(solution)/shard_map/ppermute | solution.py:322

commit v7 on v6

--- a/solution.py
+++ b/solution.py
@@ -30,7 +30,7 @@
 
 def bucket_kernel(live, *refs):
     sources, out, staged = refs[:7], refs[7], refs[8:15]
-    shifts, pieces, chosen, counts, left, right, arrivals = refs[15:]
+    shifts, pieces, chosen, counts, arrivals = refs[15:]
     copies = [
         pltpu.make_async_copy(source, place, arrivals.at[number])
         for number, (source, place) in enumerate(zip(sources, staged, strict=True))
@@ -70,27 +70,29 @@
     for number, piece in enumerate(held):
         pieces[number] = piece
     base = jnp.zeros((SLABS, LANES), jnp.float32)
-    pair = lax.broadcasted_iota(jnp.int32, (SLABS // 2, LANES), 0)
-    low = lax.broadcasted_iota(jnp.int32, (2 * LANES, LANES), 0)
+    low = lax.broadcasted_iota(jnp.int32, (LANES, LANES), 0)
+    lefts, rights, sent = [], [], 0.0
     for k in range(ROWS):
         target = dest[k : k + 1, :]
         found = counts[k * SLABS : (k + 1) * SLABS, :]
-        rank = jnp.sum(
-            jnp.where(slab == target, found[:, :LANES] + base, 0.0), axis=0, keepdims=True
+        mask = slab == target
+        rank = jnp.sum(jnp.where(mask, found[:, :LANES] + base, 0.0), axis=0, keepdims=True)
+        base = base + found[:, LANES:]
+        rights.append(jnp.where(low == rank.astype(jnp.int32), 1.0, 0.0).astype(jnp.bfloat16))
+        lefts.append(
+            jnp.concatenate(
+                [jnp.where(mask, pieces[number, k : k + 1, :], 0.0) for number in range(PIECES)], axis=0
+            ).astype(jnp.bfloat16)
         )
-        base = base + found[:, LANES:]
-        slot = jnp.right_shift(target, 5) * LANES + rank.astype(jnp.int32)
-        span = slice(k * LANES, (k + 1) * LANES)
-        right[:, span] = jnp.where(low == slot, 1.0, 0.0).astype(jnp.bfloat16)
-        mask = pair == jnp.bitwise_and(target, SLABS // 2 - 1)
-        for number in range(PIECES):
-            left[number * ROWS : (number + 1) * ROWS, span] = jnp.where(
-                mask, pieces[number, k : k + 1, :], 0.0
-            ).astype(jnp.bfloat16)
-    sent = lax.dot_general(
-        left[...], right[...], (((1,), (1,)), ((), ())), preferred_element_type=jnp.float32
-    )
-    part = [sent[number * ROWS : (number + 1) * ROWS] for number in range(PIECES)]
+        if len(lefts) == 8:
+            sent = sent + lax.dot_general(
+                jnp.concatenate(lefts, axis=1),
+                jnp.concatenate(rights, axis=1),
+                (((1,), (1,)), ((), ())),
+                preferred_element_type=jnp.float32,
+            )
+            lefts, rights = [], []
+    part = [sent[number * SLABS : (number + 1) * SLABS] for number in range(PIECES)]
     bins = jnp.floor(part[0] * (1.0 / PLANES))
     values = [
         (part[0] - PLANES * bins) + (part[3] + part[4]),
@@ -100,9 +102,7 @@
         1.0 + 0.5 * bins,
     ]
     for field, value in enumerate(values):
-        span = slice(field * LANES, (field + 1) * LANES)
-        out[: SLABS // 2, 0, span] = value[:, :LANES]
-        out[SLABS // 2 :, 0, span] = value[:, LANES:]
+        out[:, 0, field * LANES : (field + 1) * LANES] = value
 
 
 def tap_sum(position, inverse):
@@ -275,8 +275,6 @@
             pltpu.VMEM((PIECES, ROWS, LANES), jnp.float32),
             pltpu.VMEM((ROWS * SLABS, LANES), jnp.bfloat16),
             pltpu.VMEM((ROWS * SLABS, 2 * LANES), jnp.float32),
-            pltpu.VMEM((PIECES * ROWS, ROWS * LANES), jnp.bfloat16),
-            pltpu.VMEM((2 * LANES, ROWS * LANES), jnp.bfloat16),
             pltpu.SemaphoreType.DMA((7,)),
         ],
         [pl.BlockSpec(memory_space=pltpu.SMEM)] + [pl.BlockSpec(memory_space=pltpu.HBM)] * 7,

time: 99.9 us -> 99.8 us (level)
  no operation moved by 1% of the time
where the time goes in v7:
time: 99.8 us; the launch traced here: 99.5 us
  blocking collectives  86 us (86%)
  Pallas kernels  11.1 us (11%)
  starting transfers between devices  1.74 us (2%)
    all_to_all x3, blocking collectives, exchanged(): lax.all_to_all(value, 'slab', split_axis=0, concat_axis=0, tiled=True)  86 us
    pallas_call x1, Pallas kernels, bucket(): call(bucket_kernel, shape(SLABS, 1, 5 * LANES), [pltpu.VMEM(value.shape,...  3.47 us
    pallas_call x1, Pallas kernels, deposit_inner(): call(inner_kernel, (shape(CY * EXT, NZ), shape(*tables.shape[1:])), [HELD...  3.12 us
    pallas_call x1, Pallas kernels, deposit_rims(): call(rim_kernel, (rim, rim), scratch, flops=5 * 10 ** 8, moved=10 ** 6)  2.84 us
  transfers between devices with their start and end apart: 2, of which 0 were waited for; matrix products, arithmetic and copies ran while one was open for 0% of the time, Pallas kernels for 3%

profile of v7, /device:TPU:6, one launch (start us, length us, event | category | flops | bytes accessed | tf_op | source)
XLA Modules:
  0.0 99.5 jit_solution(3358300631909507197)
XLA Ops:
  0.7 3.5 %shard_map.100 = f32[64,1,640]{2,1,0:T(1,128)S(1)} custom-call(s32[1]{0:T(128)S(6)} %copy.11.live, s32[32,128]{1,0:T(8,128)} %bitcast.7, f32[3,4096]{1,0:T(4,128)} %refs_1_.1, s32[32,128]{1,0:T(8,128)} %bitcast.8, s32[32,128]{1,0:T(8,128)} %bitcast.9, s32[32,128]{1,0:T(8,128)} %bitcast.10, s32[32,128]{1,0:T(8,128)} %bitcast.11, f32[32,128]{1,0:T(8,128)} %bitcast.12), custom_call_target="tpu_custom_call" | custom-call | flops 1000000000 | bytes 1000000 | tf_op jit(solution)/shard_map/pallas_call | solution.py:269
  4.1 35.5 %all_to_all.15.arrived = f32[64,1,640]{2,1,0:T(1,128)S(1)} all-to-all(f32[64,1,640]{2,1,0:T(1,128)S(1)} %shard_map.100), channel_id=1, replica_groups=mesh['slab'=64,'pencil'=8] {'slab'}, dimensions={0} | all-to-all | bytes 327680 | tf_op jit(solution)/shard_map/all_to_all | solution.py:308
  39.6 2.8 %shard_map.102 = (f32[120,128]{1,0:T(8,128)S(1)}, f32[120,128]{1,0:T(8,128)S(1)}) custom-call(f32[64,1,640]{2,1,0:T(1,128)S(1)} %all_to_all.15.arrived), custom_call_target="tpu_custom_call" | custom-call | flops 500000000 | bytes 1000000 | tf_op jit(solution)/shard_map/pallas_call | solution.py:292
  42.5 0.0 collective-permute-start
  42.5 0.0 copy-start
  42.5 1.7 %collective-permute-start.1 = (f32[120,128]{1,0:T(8,128)S(1)}, f32[120,128]{1,0:T(8,128)S(1)}, u32[]{:S(2)}, u32[]{:S(2)}) collective-permute-start(f32[120,128]{1,0:T(8,128)S(1)} %get-tuple-element.12), channel_id=1, source_target_pairs={{1,0},{2,1},{3,2},{4,3},{5,4},{6,5},{7,6},{0,7},{9,8},{10,9},{11,1... | collective-permute-start | bytes 184328 | tf_op jit(solution)/shard_map/ppermute | solution.py:320
  44.2 3.1 %shard_map.101 = (f32[320,128]{1,0:T(8,128)S(1)}, f32[4,128,64]{2,1,0:T(8,128)S(1)}) custom-call(f32[64,1,640]{2,1,0:T(1,128)S(1)} %all_to_all.15.arrived, f32[8,4,128,64]{3,2,1,0:T(8,128)} %constant.4.clone.tables), custom_call_target="tpu_custom_call" | custom-call | flops 1000000000 | bytes 1000000 | tf_op jit(solution)/shard_map/pallas_call | solution.py:297
  47.4 0.0 collective-permute-done.before
  47.4 0.0 collective-permute-done.1.after
  47.4 0.1 shard_map.103
  47.5 23.8 %all_to_all.16.value = f32[64,1,640]{2,1,0:T(1,128)S(1)} all-to-all(f32[64,1,640]{2,1,0:T(1,128)S(1)} %shard_map.103), channel_id=1, replica_groups=mesh['slab'=64,'pencil'=8] {'slab'}, dimensions={0} | all-to-all | bytes 327680 | tf_op jit(solution)/shard_map/all_to_all | solution.py:308
  71.3 0.4 shard_map.104
  71.7 26.7 %all_to_all.17.value = f32[64,8,128]{2,1,0:T(8,128)S(1)} all-to-all(f32[64,8,128]{2,1,0:T(8,128)S(1)} %shard_map.104), channel_id=1, replica_groups=mesh['slab'=64,'pencil'=8] {'slab'}, dimensions={0} | all-to-all | bytes 524288 | tf_op jit(solution)/shard_map/all_to_all | solution.py:308
  98.4 0.0 copy-done
  98.4 1.1 %shard_map.105 = f32[64,8,128]{2,1,0:T(8,128)} custom-call(f32[64,64]{1,0:T(8,128)S(1)} %copy-done, f32[64,8,128]{2,1,0:T(8,128)S(1)} %all_to_all.17.value), custom_call_target="tpu_custom_call" | custom-call | tf_op jit(solution)/shard_map/pallas_call | solution.py:326
Async XLA Ops:
  42.5 4.9 %collective-permute-start = (f32[120,128]{1,0:T(8,128)S(1)}, f32[120,128]{1,0:T(8,128)S(1)}, u32[]{:S(2)}, u32[]{:S(2)}) collective-permute-start(f32[120,128]{1,0:T(8,128)S(1)} %get-tuple-element.11), channel_id=1, source_target_pairs={{0,1},{1,2},{2,3},{3,4},{4,5},{5,6},{6,7},{7,0},{8,9},{9,10},{10,1... | collective-permute-start | bytes 184328 | tf_op jit(solution)/shard_map/ppermute | solution.py:319
  42.5 55.9 %copy-start = (f32[64,64]{1,0:T(8,128)S(1)}, f32[64,64]{1,0:T(8,128)}, u32[]{:S(2)}) copy-start(f32[64,64]{1,0:T(8,128)} %constant.5.clone.table) | copy-start | bytes 49156
  42.5 4.9 %collective-permute-start.1 = (f32[120,128]{1,0:T(8,128)S(1)}, f32[120,128]{1,0:T(8,128)S(1)}, u32[]{:S(2)}, u32[]{:S(2)}) collective-permute-start(f32[120,128]{1,0:T(8,128)S(1)} %get-tuple-element.12), channel_id=1, source_target_pairs={{1,0},{2,1},{3,2},{4,3},{5,4},{6,5},{7,6},{0,7},{9,8},{10,9},{11,1... | collective-permute-start | bytes 184328 | tf_op jit(solution)/shard_map/ppermute | solution.py:320

commit v8 on v7

--- a/solution.py
+++ b/solution.py
@@ -128,7 +128,44 @@
 BLOCK = 16
 
 
-def deposit_rows(arrived, held, total, wanted):
+def add_rows(held, depth, fill, total, wanted):
+    total[...] = jnp.zeros_like(total)
+    wide = BLOCK * LANES
+    first = lax.broadcasted_iota(jnp.int32, (EXT, wide), 0).astype(jnp.float32) + (0.5 - GHOST)
+    second = lax.broadcasted_iota(jnp.int32, (16, wide), 0).astype(jnp.float32) + (0.5 - GHOST)
+    third = lax.broadcasted_iota(jnp.int32, (NZ, wide), 0).astype(jnp.float32) + 0.5
+
+    def step(index, carry):
+        def row(field):
+            return jnp.concatenate(
+                [held[field, pl.ds(index * BLOCK + part, 1), :] for part in range(BLOCK)], axis=1
+            )
+
+        span = pl.ds(pl.multiple_of(index * wide, wide), wide)
+        scale = row(3)
+        along_first = bump_of((first - row(0)) * scale) * row(4)
+        along_second = bump_of((second - row(1)) * scale)
+        if fill:
+            away = third - row(2)
+            away = jnp.concatenate(
+                [around(away[:8]), away[8 : NZ - 8], around(away[NZ - 8 :])], axis=0
+            )
+            along_third = (bump_of(away * scale) * row(5)).astype(jnp.bfloat16)
+            depth[:, span] = along_third
+        else:
+            along_third = depth[:, span]
+        plane = jnp.concatenate(
+            [along_first * along_second[y : y + 1, :] for y in wanted], axis=0
+        ).astype(jnp.bfloat16)
+        total[...] += lax.dot_general(
+            plane, along_third, (((1,), (1,)), ((), ())), preferred_element_type=jnp.float32
+        )
+        return carry
+
+    lax.fori_loop(0, SLABS // BLOCK, step, 0, unroll=2)
+
+
+def rim_kernel(arrived, lower, upper, held, depth, total):
     def field(number):
         return arrived[:, 0, number * LANES : (number + 1) * LANES]
 
@@ -139,45 +176,15 @@
     held[3] = inverse
     held[4] = field(3) / (tap_sum(held[0], inverse) * tap_sum(held[1], inverse))
     held[5] = 1.0 / tap_sum(held[2], inverse)
-    total[...] = jnp.zeros_like(total)
-    wide = BLOCK * LANES
-    first = lax.broadcasted_iota(jnp.int32, (EXT, wide), 0).astype(jnp.float32) + (0.5 - GHOST)
-    second = lax.broadcasted_iota(jnp.int32, (16, wide), 0).astype(jnp.float32) + (0.5 - GHOST)
-    third = lax.broadcasted_iota(jnp.int32, (NZ, wide), 0).astype(jnp.float32) + 0.5
-
-    def step(index, carry):
-        def row(field):
-            return jnp.concatenate(
-                [held[field, pl.ds(index * BLOCK + part, 1), :] for part in range(BLOCK)], axis=1
-            )
-
-        scale = row(3)
-        along_first = bump_of((first - row(0)) * scale) * row(4)
-        along_second = bump_of((second - row(1)) * scale)
-        away = third - row(2)
-        away = jnp.concatenate([around(away[:8]), away[8 : NZ - 8], around(away[NZ - 8 :])], axis=0)
-        depth = (bump_of(away * scale) * row(5)).astype(jnp.bfloat16)
-        plane = jnp.concatenate(
-            [along_first * along_second[y : y + 1, :] for y in wanted], axis=0
-        ).astype(jnp.bfloat16)
-        total[...] += lax.dot_general(
-            plane, depth, (((1,), (1,)), ((), ())), preferred_element_type=jnp.float32
-        )
-        return carry
-
-    lax.fori_loop(0, SLABS // BLOCK, step, 0, unroll=2)
-
-
-def rim_kernel(arrived, lower, upper, held, total):
-    deposit_rows(arrived, held, total, [*range(GHOST), *range(GHOST + CY, WIDE)])
+    add_rows(held, depth, True, total, [*range(GHOST), *range(GHOST + CY, WIDE)])
     lower[...] = total[: GHOST * EXT]
     upper[...] = total[GHOST * EXT :]
 
 
-def inner_kernel(arrived, tables, inner, table, held, arrival):
+def inner_kernel(held, depth, tables, inner, table, arrival):
     copy = pltpu.make_async_copy(tables.at[lax.axis_index("slab") % 8], table, arrival)
     copy.start()
-    deposit_rows(arrived, held, inner, range(GHOST, GHOST + CY))
+    add_rows(held, depth, False, inner, range(GHOST, GHOST + CY))
     copy.wait()
 
 
@@ -283,25 +290,29 @@
     )(live_counts, *[pltpu.with_memory_space_constraint(value, pltpu.HBM) for value in sources])
 
 
-HELD = pltpu.VMEM((6, SLABS, LANES), jnp.float32)
-
-
 def deposit_rims(arrived):
     rim = shape(GHOST * EXT, NZ)
-    scratch = [HELD, pltpu.VMEM((2 * GHOST * EXT, NZ), jnp.float32)]
-    return call(rim_kernel, (rim, rim), scratch, flops=5 * 10**8, moved=10**6)(arrived)
-
-
-def deposit_inner(arrived):
+    depth = jax.ShapeDtypeStruct((NZ, SLABS * LANES), jnp.bfloat16)
+    return call(
+        rim_kernel,
+        (rim, rim, shape(6, SLABS, LANES), depth),
+        [pltpu.VMEM((2 * GHOST * EXT, NZ), jnp.float32)],
+        flops=5 * 10**8,
+        moved=10**6,
+    )(arrived)
+
+
+def deposit_inner(held, depth):
     tables = pltpu.with_memory_space_constraint(jnp.asarray(slab_tables()), pltpu.HBM)
+    here = pl.BlockSpec(memory_space=pltpu.VMEM)
     return call(
         inner_kernel,
         (shape(CY * EXT, NZ), shape(*tables.shape[1:])),
-        [HELD, pltpu.SemaphoreType.DMA],
-        [pl.BlockSpec(memory_space=pltpu.VMEM), pl.BlockSpec(memory_space=pltpu.HBM)],
+        [pltpu.SemaphoreType.DMA],
+        [here, here, pl.BlockSpec(memory_space=pltpu.HBM)],
         flops=10**9,
         moved=10**6,
-    )(arrived, tables)
+    )(held, depth, tables)
 
 
 def exchanged(value):
@@ -313,12 +324,12 @@
         live_counts, cell_x, cell_y, cell_z, offsets, radius_bin, masses, slab_dest
     )
     arrived = exchanged(outgoing)
-    lower, upper = deposit_rims(arrived)
+    lower, upper, held, depth = deposit_rims(arrived)
     count = lax.axis_size("pencil")
     up = [(i, (i + 1) % count) for i in range(count)]
     before = lax.ppermute(upper, "pencil", up)
     after = lax.ppermute(lower, "pencil", [(j, i) for i, j in up])
-    inner, table = deposit_inner(arrived)
+    inner, table = deposit_inner(held, depth)
     joined = call(join_kernel, shape(SLABS, 1, GROUPS * LANES))(inner, before, after)
     crossing = exchanged(joined)
     partial = call(slab_kernel, shape(SLABS, 2 * (GROUPS - 1), LANES))(table, crossing)

time: 99.8 us -> 99.9 us (level)
  Pallas kernels: 11.1 us -> 9.89 us
  blocking collectives: 86 us -> 87.1 us
    pallas_call x2, Pallas kernels: 5.96 us -> 4.79 us  [the longest x1 3.01 us: deposit_rims(): call(rim_kernel, (rim, rim, shape(6, SLABS, LANES), depth), [pltpu.VMEM((...]
    all_to_all x3, blocking collectives: 86 us -> 87.1 us  [exchanged(): lax.all_to_all(value, 'slab', split_axis=0, concat_axis=0, tiled=True)]
  transfers between devices with their start and end apart: 2 -> 2, of which waited for: 0 -> 1; matrix products, arithmetic and copies ran while one was open for 0% -> 0% of each run, Pallas kernels for 3% -> 2%
where the time goes in v8:
time: 99.9 us; the launch traced here: 99.5 us
  blocking collectives  87.1 us (87%)
  Pallas kernels  9.89 us (10%)
  starting transfers between devices  1.75 us (2%)
    all_to_all x3, blocking collectives, exchanged(): lax.all_to_all(value, 'slab', split_axis=0, concat_axis=0, tiled=True)  87.1 us
    pallas_call x1, Pallas kernels, bucket(): call(bucket_kernel, shape(SLABS, 1, 5 * LANES), [pltpu.VMEM(value.shape,...  3.47 us
    pallas_call x1, Pallas kernels, deposit_rims(): call(rim_kernel, (rim, rim, shape(6, SLABS, LANES), depth), [pltpu.VMEM((...  3.01 us
  transfers between devices with their start and end apart: 2, of which 1 were waited for; matrix products, arithmetic and copies ran while one was open for 0% of the time, Pallas kernels for 2%

profile of v8, /device:TPU:6, one launch (start us, length us, event | category | flops | bytes accessed | tf_op | source)
XLA Modules:
  0.0 99.5 jit_solution(17928424724466328141)
XLA Ops:
  0.7 3.5 %shard_map.100 = f32[64,1,640]{2,1,0:T(1,128)S(1)} custom-call(s32[1]{0:T(128)S(6)} %copy.11.live, s32[32,128]{1,0:T(8,128)} %bitcast.7, f32[3,4096]{1,0:T(4,128)} %refs_1_.1, s32[32,128]{1,0:T(8,128)} %bitcast.8, s32[32,128]{1,0:T(8,128)} %bitcast.9, s32[32,128]{1,0:T(8,128)} %bitcast.10, s32[32,128]{1,0:T(8,128)} %bitcast.11, f32[32,128]{1,0:T(8,128)} %bitcast.12), custom_call_target="tpu_custom_call" | custom-call | flops 1000000000 | bytes 1000000 | tf_op jit(solution)/shard_map/pallas_call | solution.py:276
  4.1 35.5 %all_to_all.15.arrived = f32[64,1,640]{2,1,0:T(1,128)S(1)} all-to-all(f32[64,1,640]{2,1,0:T(1,128)S(1)} %shard_map.100), channel_id=1, replica_groups=mesh['slab'=64,'pencil'=8] {'slab'}, dimensions={0} | all-to-all | bytes 327680 | tf_op jit(solution)/shard_map/all_to_all | solution.py:319
  39.6 3.0 %shard_map.101 = (f32[120,128]{1,0:T(8,128)S(1)}, f32[120,128]{1,0:T(8,128)S(1)}, f32[6,64,128]{2,1,0:T(8,128)S(1)}, bf16[128,8192]{1,0:T(8,128)(2,1)S(1)}) custom-call(f32[64,1,640]{2,1,0:T(1,128)S(1)} %all_to_all.15.arrived), custom_call_target="tpu_custom_call" | custom-call | flops 500000000 | bytes 1000000 | tf_op jit(solution)/shard_map/pallas_call | solution.py:296
  42.7 0.0 collective-permute-start
  42.7 1.7 %collective-permute-start.1 = (f32[120,128]{1,0:T(8,128)S(1)}, f32[120,128]{1,0:T(8,128)S(1)}, u32[]{:S(2)}, u32[]{:S(2)}) collective-permute-start(f32[120,128]{1,0:T(8,128)S(1)} %get-tuple-element.16), channel_id=1, source_target_pairs={{1,0},{2,1},{3,2},{4,3},{5,4},{6,5},{7,6},{0,7},{9,8},{10,9},{11,1... | collective-permute-start | bytes 184328 | tf_op jit(solution)/shard_map/ppermute | solution.py:331
  44.4 0.0 copy-start
  44.4 1.8 %shard_map.102 = (f32[320,128]{1,0:T(8,128)S(1)}, f32[4,128,64]{2,1,0:T(8,128)S(1)}) custom-call(f32[6,64,128]{2,1,0:T(8,128)S(1)} %get-tuple-element.11.held, bf16[128,8192]{1,0:T(8,128)(2,1)S(1)} %get-tuple-element.12.depth, f32[8,4,128,64]{3,2,1,0:T(8,128)} %constant.4.clone.tables), custom_call_target="tpu_custom_call" | custom-call | flops 1000000000 | bytes 1000000 | tf_op jit(solution)/shard_map/pallas_call | solution.py:308
  46.2 0.1 collective-permute-done.before
  46.3 0.0 collective-permute-done.1.after
  46.3 0.1 shard_map.103
  46.4 23.7 %all_to_all.16.value = f32[64,1,640]{2,1,0:T(1,128)S(1)} all-to-all(f32[64,1,640]{2,1,0:T(1,128)S(1)} %shard_map.103), channel_id=1, replica_groups=mesh['slab'=64,'pencil'=8] {'slab'}, dimensions={0} | all-to-all | bytes 327680 | tf_op jit(solution)/shard_map/all_to_all | solution.py:319
  70.1 0.4 shard_map.104
  70.5 27.9 %all_to_all.17.value = f32[64,8,128]{2,1,0:T(8,128)S(1)} all-to-all(f32[64,8,128]{2,1,0:T(8,128)S(1)} %shard_map.104), channel_id=1, replica_groups=mesh['slab'=64,'pencil'=8] {'slab'}, dimensions={0} | all-to-all | bytes 524288 | tf_op jit(solution)/shard_map/all_to_all | solution.py:319
  98.4 0.0 copy-done
  98.4 1.1 %shard_map.105 = f32[64,8,128]{2,1,0:T(8,128)} custom-call(f32[64,64]{1,0:T(8,128)S(1)} %copy-done, f32[64,8,128]{2,1,0:T(8,128)S(1)} %all_to_all.17.value), custom_call_target="tpu_custom_call" | custom-call | tf_op jit(solution)/shard_map/pallas_call | solution.py:337
Async XLA Ops:
  42.7 3.7 %collective-permute-start = (f32[120,128]{1,0:T(8,128)S(1)}, f32[120,128]{1,0:T(8,128)S(1)}, u32[]{:S(2)}, u32[]{:S(2)}) collective-permute-start(f32[120,128]{1,0:T(8,128)S(1)} %get-tuple-element.15), channel_id=1, source_target_pairs={{0,1},{1,2},{2,3},{3,4},{4,5},{5,6},{6,7},{7,0},{8,9},{9,10},{10,1... | collective-permute-start | bytes 184328 | tf_op jit(solution)/shard_map/ppermute | solution.py:330
  42.7 3.6 %collective-permute-start.1 = (f32[120,128]{1,0:T(8,128)S(1)}, f32[120,128]{1,0:T(8,128)S(1)}, u32[]{:S(2)}, u32[]{:S(2)}) collective-permute-start(f32[120,128]{1,0:T(8,128)S(1)} %get-tuple-element.16), channel_id=1, source_target_pairs={{1,0},{2,1},{3,2},{4,3},{5,4},{6,5},{7,6},{0,7},{9,8},{10,9},{11,1... | collective-permute-start | bytes 184328 | tf_op jit(solution)/shard_map/ppermute | solution.py:331
  44.4 54.0 %copy-start = (f32[64,64]{1,0:T(8,128)S(1)}, f32[64,64]{1,0:T(8,128)}, u32[]{:S(2)}) copy-start(f32[64,64]{1,0:T(8,128)} %constant.5.clone.table) | copy-start | bytes 49156

commit v9 on v7

--- a/solution.py
+++ b/solution.py
@@ -84,7 +84,7 @@
                 [jnp.where(mask, pieces[number, k : k + 1, :], 0.0) for number in range(PIECES)], axis=0
             ).astype(jnp.bfloat16)
         )
-        if len(lefts) == 8:
+        if len(lefts) == 4:
             sent = sent + lax.dot_general(
                 jnp.concatenate(lefts, axis=1),
                 jnp.concatenate(rights, axis=1),

time: 99.8 us -> 99.8 us (level)
  no operation moved by 1% of the time
where the time goes in v9:
time: 99.8 us; the launch traced here: 99.5 us
  blocking collectives  86 us (86%)
  Pallas kernels  11.1 us (11%)
  starting transfers between devices  1.74 us (2%)
    all_to_all x3, blocking collectives, exchanged(): lax.all_to_all(value, 'slab', split_axis=0, concat_axis=0, tiled=True)  86 us
    pallas_call x1, Pallas kernels, bucket(): call(bucket_kernel, shape(SLABS, 1, 5 * LANES), [pltpu.VMEM(value.shape,...  3.49 us
    pallas_call x1, Pallas kernels, deposit_inner(): call(inner_kernel, (shape(CY * EXT, NZ), shape(*tables.shape[1:])), [HELD...  3.12 us
    pallas_call x1, Pallas kernels, deposit_rims(): call(rim_kernel, (rim, rim), scratch, flops=5 * 10 ** 8, moved=10 ** 6)  2.84 us
  transfers between devices with their start and end apart: 2, of which 0 were waited for; matrix products, arithmetic and copies ran while one was open for 0% of the time, Pallas kernels for 3%

profile of v9, /device:TPU:6, one launch (start us, length us, event | category | flops | bytes accessed | tf_op | source)
XLA Modules:
  0.0 99.5 jit_solution(7274215307399829307)
XLA Ops:
  0.7 3.5 %shard_map.100 = f32[64,1,640]{2,1,0:T(1,128)S(1)} custom-call(s32[1]{0:T(128)S(6)} %copy.11.live, s32[32,128]{1,0:T(8,128)} %bitcast.7, f32[3,4096]{1,0:T(4,128)} %refs_1_.1, s32[32,128]{1,0:T(8,128)} %bitcast.8, s32[32,128]{1,0:T(8,128)} %bitcast.9, s32[32,128]{1,0:T(8,128)} %bitcast.10, s32[32,128]{1,0:T(8,128)} %bitcast.11, f32[32,128]{1,0:T(8,128)} %bitcast.12), custom_call_target="tpu_custom_call" | custom-call | flops 1000000000 | bytes 1000000 | tf_op jit(solution)/shard_map/pallas_call | solution.py:269
  4.2 35.5 %all_to_all.15.arrived = f32[64,1,640]{2,1,0:T(1,128)S(1)} all-to-all(f32[64,1,640]{2,1,0:T(1,128)S(1)} %shard_map.100), channel_id=1, replica_groups=mesh['slab'=64,'pencil'=8] {'slab'}, dimensions={0} | all-to-all | bytes 327680 | tf_op jit(solution)/shard_map/all_to_all | solution.py:308
  39.7 2.8 %shard_map.102 = (f32[120,128]{1,0:T(8,128)S(1)}, f32[120,128]{1,0:T(8,128)S(1)}) custom-call(f32[64,1,640]{2,1,0:T(1,128)S(1)} %all_to_all.15.arrived), custom_call_target="tpu_custom_call" | custom-call | flops 500000000 | bytes 1000000 | tf_op jit(solution)/shard_map/pallas_call | solution.py:292
  42.5 0.0 collective-permute-start
  42.5 0.0 copy-start
  42.5 1.7 %collective-permute-start.1 = (f32[120,128]{1,0:T(8,128)S(1)}, f32[120,128]{1,0:T(8,128)S(1)}, u32[]{:S(2)}, u32[]{:S(2)}) collective-permute-start(f32[120,128]{1,0:T(8,128)S(1)} %get-tuple-element.12), channel_id=1, source_target_pairs={{1,0},{2,1},{3,2},{4,3},{5,4},{6,5},{7,6},{0,7},{9,8},{10,9},{11,1... | collective-permute-start | bytes 184328 | tf_op jit(solution)/shard_map/ppermute | solution.py:320
  44.3 3.1 %shard_map.101 = (f32[320,128]{1,0:T(8,128)S(1)}, f32[4,128,64]{2,1,0:T(8,128)S(1)}) custom-call(f32[64,1,640]{2,1,0:T(1,128)S(1)} %all_to_all.15.arrived, f32[8,4,128,64]{3,2,1,0:T(8,128)} %constant.4.clone.tables), custom_call_target="tpu_custom_call" | custom-call | flops 1000000000 | bytes 1000000 | tf_op jit(solution)/shard_map/pallas_call | solution.py:297
  47.4 0.0 collective-permute-done.before
  47.4 0.0 collective-permute-done.1.after
  47.4 0.1 shard_map.103
  47.5 23.8 %all_to_all.16.value = f32[64,1,640]{2,1,0:T(1,128)S(1)} all-to-all(f32[64,1,640]{2,1,0:T(1,128)S(1)} %shard_map.103), channel_id=1, replica_groups=mesh['slab'=64,'pencil'=8] {'slab'}, dimensions={0} | all-to-all | bytes 327680 | tf_op jit(solution)/shard_map/all_to_all | solution.py:308
  71.3 0.4 shard_map.104
  71.8 26.7 %all_to_all.17.value = f32[64,8,128]{2,1,0:T(8,128)S(1)} all-to-all(f32[64,8,128]{2,1,0:T(8,128)S(1)} %shard_map.104), channel_id=1, replica_groups=mesh['slab'=64,'pencil'=8] {'slab'}, dimensions={0} | all-to-all | bytes 524288 | tf_op jit(solution)/shard_map/all_to_all | solution.py:308
  98.4 0.0 copy-done
  98.4 1.1 %shard_map.105 = f32[64,8,128]{2,1,0:T(8,128)} custom-call(f32[64,64]{1,0:T(8,128)S(1)} %copy-done, f32[64,8,128]{2,1,0:T(8,128)S(1)} %all_to_all.17.value), custom_call_target="tpu_custom_call" | custom-call | tf_op jit(solution)/shard_map/pallas_call | solution.py:326
Async XLA Ops:
  42.5 4.9 %collective-permute-start = (f32[120,128]{1,0:T(8,128)S(1)}, f32[120,128]{1,0:T(8,128)S(1)}, u32[]{:S(2)}, u32[]{:S(2)}) collective-permute-start(f32[120,128]{1,0:T(8,128)S(1)} %get-tuple-element.11), channel_id=1, source_target_pairs={{0,1},{1,2},{2,3},{3,4},{4,5},{5,6},{6,7},{7,0},{8,9},{9,10},{10,1... | collective-permute-start | bytes 184328 | tf_op jit(solution)/shard_map/ppermute | solution.py:319
  42.5 55.9 %copy-start = (f32[64,64]{1,0:T(8,128)S(1)}, f32[64,64]{1,0:T(8,128)}, u32[]{:S(2)}) copy-start(f32[64,64]{1,0:T(8,128)} %constant.5.clone.table) | copy-start | bytes 49156
  42.5 4.9 %collective-permute-start.1 = (f32[120,128]{1,0:T(8,128)S(1)}, f32[120,128]{1,0:T(8,128)S(1)}, u32[]{:S(2)}, u32[]{:S(2)}) collective-permute-start(f32[120,128]{1,0:T(8,128)S(1)} %get-tuple-element.12), channel_id=1, source_target_pairs={{1,0},{2,1},{3,2},{4,3},{5,4},{6,5},{7,6},{0,7},{9,8},{10,9},{11,1... | collective-permute-start | bytes 184328 | tf_op jit(solution)/shard_map/ppermute | solution.py:320
